TPU v7x, 32 devices: a whole 2x2x4 slice. The times are simulated.
32 devices in a mesh: gx: 2 (over x), gy: 4 (over z), gz: 4 (over y, core).
Axes of the slice: x: 2, y: 2, z: 4, core: 2. Of those that a mesh axis runs over, the one named last changes fastest.
Arguments:
- pressure: float32 [2, 32, 32, 512], P(None, 'gx', 'gy', 'gz'), may hold values from -6 to 6
- saturation: float32 [3, 2, 32, 32, 512], P(None, None, 'gx', 'gy', 'gz'), may hold values from 0.15 to 0.45
- permeability: float32 [32, 32, 512], P('gx', 'gy', 'gz'), may hold values from 0.5 to 2
- porosity: float32 [32, 32, 512], P('gx', 'gy', 'gz'), may hold values from 0.1 to 0.35
- upwind_flags: int32 [32, 32, 512], P('gx', 'gy', 'gz'), may hold values from 0 to 63
- diag_inverse: float32 [2, 3, 3, 32, 32, 512], P(None, None, None, 'gx', 'gy', 'gz'), may hold values from -0.12 to 0.8, as said below
- seismic_obs: float32 [32, 32, 512], P('gx', 'gy', 'gz'), may hold values from -6 to 6
- well_x: int32 [2, 4, 64], P('gx', 'gy'), may hold values from 0 to 15
- well_y: int32 [2, 4, 64], P('gx', 'gy'), may hold values from 0 to 7
- well_top: int32 [2, 4, 64], P('gx', 'gy'), may hold values from 0 to 255
- well_len: int32 [2, 4, 64], P('gx', 'gy'), may hold values from 128 to 256
- well_bhp: float32 [2, 2, 4, 64], P(None, 'gx', 'gy'), may hold values from -3 to 3
- well_obs: float32 [2, 2, 4, 64], P(None, 'gx', 'gy'), may hold values from -48 to 48
- fault_cell: int32 [32, 16, 128], P(('gx', 'gy', 'gz')), may hold values from 0 to 16383
- fault_count: int32 [32, 16], P(('gx', 'gy', 'gz')), may hold values from 0 to 128, as said below
- fault_trans: float32 [32, 16, 128], P(('gx', 'gy', 'gz')), may hold values from 0.5 to 2, as said below
- fault_up: int32 [32, 16, 128], P(('gx', 'gy', 'gz')), may hold values from 0 to 3, as said below
- region_map: int32 [8, 8, 128], P('gx', 'gy', 'gz'), may hold values from 0 to 1023
Outputs:
- adjoint: float32 [2, 3, 32, 32, 512], P(None, None, 'gx', 'gy', 'gz')
- region_grad: float32 [2, 1024], P(None, ('gx', 'gy', 'gz'))
Inputs may be any that keep to these rules, and one draw needn't show every extreme that they name: fault_count[dev][p] equals fault_count[i * 16 + p][a] of the connection's other end; a device has no connections with itself; in every draw one device of each group of 16 has exactly 128 connections with every other device of its group. `fault_cell`: slot s of dev toward peer p and slot s of that peer toward dev are the two ends of one connection. `fault_trans`: both ends of a connection hold the same transmissibility. `fault_up`: the two ends of a connection hold opposite bits. `diag_inverse`: entries [t][0][0] lie in 0.25 to 0.5, entries [t][u][u] for u = 1, 2 in 0.4 to 0.8, all others in -0.12 to 0.12.
All inputs are finite; a program needn't handle non-finite values.
Results may differ from a plain program's by a relative error of at most 0.0001.
Values sent between devices are 32-bit elements; how exact they have to be, the bound alone decides.
A program may use at most 128 MiB of HBM per device.

v0:
```python
import jax
import jax.numpy as jnp
from jax import lax
from jax.sharding import PartitionSpec as P

ITERS = 6
BOX = 4
PARAM_REGIONS = 32
fluid_viscosity = (0.4, 0.5, 1.0)
sigma_sq = 64.0


def extended_2(block, sides, width):
    for axis, dim in sides:
        count = lax.axis_size(axis)
        forward = [(i, i + 1) for i in range(count - 1)]
        backward = [(target, source) for source, target in forward]
        low = lax.ppermute(
            lax.slice_in_dim(block, block.shape[dim] - width, None, axis=dim), axis, forward
        )
        high = lax.ppermute(lax.slice_in_dim(block, 0, width, axis=dim), axis, backward)
        block = jnp.concatenate([low, block, high], axis=dim)
    return block


def phase_mobility(water_sat, oil_sat):
    gas_sat = 1.0 - water_sat - oil_sat
    return jnp.stack(
        [
            water_sat * water_sat / fluid_viscosity[0],
            oil_sat * oil_sat / fluid_viscosity[1],
            gas_sat * gas_sat / fluid_viscosity[2],
        ]
    )


def mobility_slopes(water_sat, oil_sat):
    gas_sat = 1.0 - water_sat - oil_sat
    return (
        2.0 * water_sat / fluid_viscosity[0] - 2.0 * gas_sat / fluid_viscosity[2],
        2.0 * oil_sat / fluid_viscosity[1] - 2.0 * gas_sat / fluid_viscosity[2],
    )


def interior_strip(padded, direction):
    slicer = [slice(None), slice(1, -1), slice(1, -1), slice(1, -1)]
    slicer[direction + 1] = slice(None)
    return padded[tuple(slicer)]


def apply_inverse(inverse, residual):
    return jnp.sum(inverse * residual[:, None], axis=0)


def box_sums(quantity):
    shaped = quantity.reshape(
        quantity.shape[0] // BOX, BOX, quantity.shape[1] // BOX, BOX, quantity.shape[2] // BOX, BOX
    )
    return jnp.sum(shaped, axis=(1, 3, 5)).reshape(-1)


def fault_exchange(values):
    return lax.all_to_all(values, ("gy", "gz"), split_axis=1, concat_axis=1, tiled=True)


def fault_sum(lagrange, coefficient, cell_index):
    flattened = lagrange.reshape(lagrange.shape[0], -1)
    own_values = flattened[:, cell_index]
    arrived = fault_exchange(own_values)
    contribution = jnp.sum(coefficient * arrived, axis=0)
    faults = (
        jnp.zeros((flattened.shape[1],), jnp.float32)
        .at[cell_index.reshape(-1)]
        .add(contribution.reshape(-1))
    )
    return faults.reshape(lagrange.shape[1:])


def neighbour_terms(lagrange, ahead_list, behind_list, want_local):
    padded = extended_2(lagrange, (("gx", 1), ("gy", 2), ("gz", 3)), 1)
    upper_terms = []
    lower_terms = []
    for direction in range(3):
        stripe = interior_strip(padded, direction)
        length = lagrange.shape[direction + 1]
        upper_terms.append(
            jnp.sum(
                ahead_list[direction] * lax.slice_in_dim(stripe, 2, length + 2, axis=direction + 1),
                axis=0,
            )
        )
        lower_terms.append(
            jnp.sum(
                behind_list[direction] * lax.slice_in_dim(stripe, 0, length, axis=direction + 1),
                axis=0,
            )
        )
    local_ahead = None
    local_behind = None
    if want_local:
        local_ahead = [jnp.sum(coefficient * lagrange, axis=0) for coefficient in ahead_list]
        local_behind = [jnp.sum(coefficient * lagrange, axis=0) for coefficient in behind_list]
    return (upper_terms, lower_terms, local_ahead, local_behind)


def local(
    pressure,
    saturation,
    permeability,
    porosity,
    upwind_flags,
    diag_inverse,
    seismic_obs,
    well_x,
    well_y,
    well_top,
    well_len,
    well_bhp,
    well_obs,
    fault_cell,
    fault_count,
    fault_trans,
    fault_up,
    region_map,
):
    mobility = [
        phase_mobility(saturation[step_index + 1, 0], saturation[step_index + 1, 1])
        for step_index in range(2)
    ]
    flag_field = upwind_flags.astype(jnp.float32)[None]
    bundle = jnp.concatenate(
        [permeability[None], mobility[0], mobility[1], flag_field, pressure], axis=0
    )
    padded = extended_2(bundle, (("gx", 1), ("gy", 2), ("gz", 3)), 1)
    ahead_coef = [[], []]
    behind_coef = [[], []]
    pressure_ahead = [[], []]
    pressure_trailing = [[], []]
    for direction in range(3):
        stripe = interior_strip(padded, direction)
        length = permeability.shape[direction]
        lower_side = lax.slice_in_dim(stripe, 0, length + 1, axis=direction + 1)
        upper_side = lax.slice_in_dim(stripe, 1, length + 2, axis=direction + 1)
        face_trans = jnp.sqrt(lower_side[0] * upper_side[0])
        lower_flags = lower_side[7].astype(jnp.int32)
        for step_index in range(2):
            first = 1 + 3 * step_index
            upwind_bit = jnp.bitwise_and(
                jnp.right_shift(lower_flags, 3 * step_index + direction), 1
            )
            chosen = jnp.where(
                upwind_bit[None] == 1, lower_side[first : first + 3], upper_side[first : first + 3]
            )
            extended = face_trans[None] * chosen
            ahead_coef[step_index].append(
                lax.slice_in_dim(extended, 1, length + 1, axis=direction + 1)
            )
            behind_coef[step_index].append(
                lax.slice_in_dim(extended, 0, length, axis=direction + 1)
            )
            pressure_stripe = stripe[8 + step_index]
            pressure_ahead[step_index].append(
                lax.slice_in_dim(pressure_stripe, 2, length + 2, axis=direction)
            )
            pressure_trailing[step_index].append(
                lax.slice_in_dim(pressure_stripe, 0, length, axis=direction)
            )
    cell_index = fault_cell[0]
    live_slots = (
        jnp.arange(cell_index.shape[1], dtype=jnp.int32)[None, :] < fault_count[0][:, None]
    ).astype(jnp.float32)
    own_mobility = jnp.concatenate(mobility, axis=0).reshape(6, -1)[:, cell_index]
    peer_mobility = lax.all_to_all(
        own_mobility, ("gy", "gz"), split_axis=1, concat_axis=1, tiled=True
    )
    fault_coef = []
    for step_index in range(2):
        upwind_bit = jnp.bitwise_and(jnp.right_shift(fault_up[0], step_index), 1)
        first = 3 * step_index
        chosen = jnp.where(
            upwind_bit[None] == 1, own_mobility[first : first + 3], peer_mobility[first : first + 3]
        )
        fault_coef.append(fault_trans[0][None] * chosen * live_slots[None])
    column_x = well_x[0, 0]
    column_y = well_y[0, 0]
    depth_count = permeability.shape[2]
    depth_index = (lax.axis_index("gz") * depth_count + jnp.arange(depth_count, dtype=jnp.int32))[
        None, :
    ]
    top_cells = well_top[0, 0][:, None]
    perforated = (
        (depth_index >= top_cells) & (depth_index < top_cells + well_len[0, 0][:, None])
    ).astype(jnp.float32)
    column_perm = permeability[column_x, column_y]
    partial_rates = []
    column_data = []
    for step_index in range(2):
        column_pressure = pressure[step_index][column_x, column_y]
        column_total = jnp.sum(mobility[step_index][:, column_x, column_y], axis=0)
        drawdown = column_pressure - well_bhp[step_index, 0, 0][:, None]
        partial_rates.append(jnp.sum(perforated * column_perm * column_total * drawdown, axis=1))
        column_data.append((column_total, drawdown))
    well_flow_rates = lax.psum(jnp.stack(partial_rates), "gz")
    misfit = (well_flow_rates - well_obs[:, 0, 0]) / sigma_sq
    sources = []
    explicit = jnp.zeros(permeability.shape, jnp.float32)
    for step_index in range(2):
        column_total, drawdown = column_data[step_index]
        water_slope, oil_slope = mobility_slopes(
            saturation[step_index + 1, 0][column_x, column_y],
            saturation[step_index + 1, 1][column_x, column_y],
        )
        weight = misfit[step_index][:, None] * column_perm * perforated
        added = jnp.stack(
            [weight * column_total, weight * drawdown * water_slope, weight * drawdown * oil_slope]
        )
        sources.append(
            jnp.zeros((3,) + permeability.shape, jnp.float32).at[:, column_x, column_y].add(added)
        )
        explicit = explicit.at[column_x, column_y].add(weight * column_total * drawdown)
    sources[1] = sources[1].at[1].add(saturation[2, 0] - seismic_obs)

    def solve(step_index, source):
        lagrange = apply_inverse(diag_inverse[step_index], source)
        for sweep_index in range(ITERS - 1):
            upper_terms, lower_terms, spare_leading, unused_behind = neighbour_terms(
                lagrange, ahead_coef[step_index], behind_coef[step_index], False
            )
            face_total = (
                upper_terms[0]
                + lower_terms[0]
                + upper_terms[1]
                + lower_terms[1]
                + upper_terms[2]
                + lower_terms[2]
            )
            coupling = face_total + fault_sum(lagrange, fault_coef[step_index], cell_index)
            residual = jnp.concatenate([(source[0] + coupling)[None], source[1:]], axis=0)
            lagrange = apply_inverse(diag_inverse[step_index], residual)
        return lagrange

    late = solve(1, sources[1])
    early_source = sources[0] + jnp.stack(
        [jnp.zeros_like(porosity), porosity * (late[0] - late[2]), porosity * (late[1] - late[2])]
    )
    early = solve(0, early_source)
    solved = [early, late]
    flux_list = []
    porosity_terms = []
    for step_index in (1, 0):
        lagrange = solved[step_index]
        upper_terms, lower_terms, local_ahead, local_behind = neighbour_terms(
            lagrange, ahead_coef[step_index], behind_coef[step_index], True
        )
        pressure_here = pressure[step_index]
        flux_grad = jnp.zeros_like(pressure_here)
        for direction in range(3):
            flux_grad = (
                flux_grad
                + 0.5
                * (pressure_here - pressure_ahead[step_index][direction])
                * (local_ahead[direction] - upper_terms[direction])
                + 0.5
                * (pressure_trailing[step_index][direction] - pressure_here)
                * (lower_terms[direction] - local_behind[direction])
            )
        flux_list.append(flux_grad)
        water_change = saturation[step_index + 1, 0] - saturation[step_index, 0]
        oil_change = saturation[step_index + 1, 1] - saturation[step_index, 1]
        porosity_terms.append(
            lagrange[0] * water_change
            + lagrange[1] * oil_change
            - lagrange[2] * (water_change + oil_change)
        )
    log_perm_grad = explicit - (flux_list[0] + flux_list[1])
    porosity_gradient = -(porosity_terms[0] + porosity_terms[1])
    box_totals = jnp.stack([box_sums(log_perm_grad), box_sums(porosity_gradient)], axis=1)
    region_labels = PARAM_REGIONS * lax.axis_size("gx") * lax.axis_size("gy") * lax.axis_size("gz")
    region_partial = jax.ops.segment_sum(
        box_totals, region_map.reshape(-1), num_segments=region_labels
    ).T
    region_grad = lax.psum_scatter(
        region_partial, ("gx", "gy", "gz"), scatter_dimension=1, tiled=True
    )
    return (jnp.stack([early, late]), region_grad)


def solution(mesh):
    placed = (
        P(None, "gx", "gy", "gz"),
        P(None, None, "gx", "gy", "gz"),
        P("gx", "gy", "gz"),
        P("gx", "gy", "gz"),
        P("gx", "gy", "gz"),
        P(None, None, None, "gx", "gy", "gz"),
        P("gx", "gy", "gz"),
        P("gx", "gy", None),
        P("gx", "gy", None),
        P("gx", "gy", None),
        P("gx", "gy", None),
        P(None, "gx", "gy", None),
        P(None, "gx", "gy", None),
        P(("gx", "gy", "gz"), None, None),
        P(("gx", "gy", "gz"), None),
        P(("gx", "gy", "gz"), None, None),
        P(("gx", "gy", "gz"), None, None),
        P("gx", "gy", "gz"),
    )
    return jax.shard_map(
        local,
        mesh=mesh,
        in_specs=placed,
        out_specs=(P(None, None, "gx", "gy", "gz"), P(None, ("gx", "gy", "gz"))),
        check_vma=False,
    )
```

profile of v0, /device:TPU:0, one launch (start us, length us, event | category | flops | bytes accessed | tf_op | source)
XLA Modules:
  0.0 1039.0 jit_solution(6294457973169037684)
XLA Ops:
  18.0 8.5 psum.7
  40.4 11.0 %gather_fusion.8 = f32[2048,3]{1,0:T(8,128)} fusion(f32[3,16384]{0,1:T(8,128)} %bitcast.380, s32[2048]{0:T(1024)S(1)} %fusion.262), kind=kCustom, calls=%fused_computation.8 | custom fusion | bytes 57344 | tf_op jit(solution)/shard_map/gather | solution.py:68
  78.6 5.3 copy.142
  83.9 11.0 %gather_fusion.7 = f32[2048,6]{1,0:T(8,128)} fusion(f32[6,16384]{0,1:T(8,128)} %copy.142, s32[2048]{0:T(1024)S(1)} %fusion.262), kind=kCustom, calls=%fused_computation.7 | custom fusion | bytes 106496 | tf_op jit(solution)/shard_map/gather | solution.py:172
  108.8 5.9 all-to-all-start
  114.7 6.8 all-to-all-done
  123.1 12.0 %scatter_custom_fusion.1 = f32[16384]{0:T(1024)} fusion(s32[2048]{0:T(1024)} %bitcast.453, f32[2048]{0:T(1024)S(1)} %bitcast.444, f32[]{:T(128)} %constant.81.clone.1), kind=kCustom, calls=%fused_computation.698 | custom fusion | flops 2048 | bytes 66048 | tf_op jit(solution)/shard_map/scatter-add | solution.py:74
  174.7 5.6 copy.182
  180.3 11.0 %gather_fusion.9 = f32[2048,3]{1,0:T(8,128)} fusion(f32[3,16384]{0,1:T(8,128)} %bitcast.383, s32[2048]{0:T(1024)S(1)} %fusion.262), kind=kCustom, calls=%fused_computation.9 | custom fusion | bytes 57344 | tf_op jit(solution)/shard_map/gather | solution.py:68
  207.4 12.0 %scatter_custom_fusion.2 = f32[16384]{0:T(1024)} fusion(s32[2048]{0:T(1024)} %bitcast.454, f32[2048]{0:T(1024)S(1)} %bitcast.447, f32[]{:T(128)} %constant.81.clone.1), kind=kCustom, calls=%fused_computation.696 | custom fusion | flops 2048 | bytes 66048 | tf_op jit(solution)/shard_map/scatter-add | solution.py:74
  236.0 5.6 copy.183
  241.6 11.0 %gather_fusion.10 = f32[2048,3]{1,0:T(8,128)} fusion(f32[3,16384]{0,1:T(8,128)} %bitcast.384, s32[2048]{0:T(1024)S(1)} %fusion.262), kind=kCustom, calls=%fused_computation.10 | custom fusion | bytes 57344 | tf_op jit(solution)/shard_map/gather | solution.py:68
  254.7 11.1 %all-to-all-start.3 = ((f32[3,16,128]{2,0,1:T(4,128)}), f32[3,16,128]{2,0,1:T(4,128)}, u32[]{:S(2)}, u32[]{:S(2)}) async-start(f32[3,16,128]{2,0,1:T(4,128)} %bitcast.436), calls=%async_computation.3 | async-start | bytes 65536 | tf_op jit(solution)/shard_map/all_to_all | solution.py:63
  275.6 12.0 %scatter_custom_fusion.3 = f32[16384]{0:T(1024)} fusion(s32[2048]{0:T(1024)} %bitcast.455, f32[2048]{0:T(1024)S(1)} %bitcast.448, f32[]{:T(128)} %constant.81.clone.1), kind=kCustom, calls=%fused_computation.694 | custom fusion | flops 2048 | bytes 66048 | tf_op jit(solution)/shard_map/scatter-add | solution.py:74
  299.0 5.3 collective-permute-start.27
  304.4 5.6 copy.184
  310.0 11.0 %gather_fusion.11 = f32[2048,3]{1,0:T(8,128)} fusion(f32[3,16384]{0,1:T(8,128)} %bitcast.385, s32[2048]{0:T(1024)S(1)} %fusion.262), kind=kCustom, calls=%fused_computation.11 | custom fusion | bytes 57344 | tf_op jit(solution)/shard_map/gather | solution.py:68
  323.1 11.2 %all-to-all-start.4 = ((f32[3,16,128]{2,0,1:T(4,128)}), f32[3,16,128]{2,0,1:T(4,128)}, u32[]{:S(2)}, u32[]{:S(2)}) async-start(f32[3,16,128]{2,0,1:T(4,128)} %bitcast.437), calls=%async_computation.4 | async-start | bytes 65536 | tf_op jit(solution)/shard_map/all_to_all | solution.py:63
  344.1 12.0 %scatter_custom_fusion.4 = f32[16384]{0:T(1024)} fusion(s32[2048]{0:T(1024)} %bitcast.456, f32[2048]{0:T(1024)S(1)} %bitcast.449, f32[]{:T(128)} %constant.81.clone.1), kind=kCustom, calls=%fused_computation.692 | custom fusion | flops 2048 | bytes 66048 | tf_op jit(solution)/shard_map/scatter-add | solution.py:74
  394.9 7.2 scatter_fusion.2
  402.1 7.2 scatter_fusion.3
  409.3 5.6 copy.185
  414.9 11.0 %gather_fusion.12 = f32[2048,3]{1,0:T(8,128)} fusion(f32[3,16384]{0,1:T(8,128)} %bitcast.386, s32[2048]{0:T(1024)S(1)} %fusion.262), kind=kCustom, calls=%fused_computation.12 | custom fusion | bytes 57344 | tf_op jit(solution)/shard_map/gather | solution.py:68
  428.0 11.1 %all-to-all-start.5 = ((f32[3,16,128]{2,0,1:T(4,128)}), f32[3,16,128]{2,0,1:T(4,128)}, u32[]{:S(2)}, u32[]{:S(2)}) async-start(f32[3,16,128]{2,0,1:T(4,128)} %bitcast.438), calls=%async_computation.5 | async-start | bytes 65536 | tf_op jit(solution)/shard_map/all_to_all | solution.py:63
  449.0 12.0 %scatter_custom_fusion.5 = f32[16384]{0:T(1024)} fusion(s32[2048]{0:T(1024)} %bitcast.457, f32[2048]{0:T(1024)S(1)} %bitcast.446, f32[]{:T(128)} %constant.81.clone.1), kind=kCustom, calls=%fused_computation.690 | custom fusion | flops 2048 | bytes 66048 | tf_op jit(solution)/shard_map/scatter-add | solution.py:74
  465.4 7.2 scatter_fusion.1
  489.4 5.6 copy.186
  496.7 11.0 %gather_fusion.15 = f32[2048,3]{1,0:T(8,128)} fusion(f32[3,16384]{0,1:T(8,128)} %bitcast.381, s32[2048]{0:T(1024)S(1)} %fusion.262), kind=kCustom, calls=%fused_computation.15 | custom fusion | bytes 57344 | tf_op jit(solution)/shard_map/gather | solution.py:68
  509.8 11.2 %all-to-all-start.6 = ((f32[3,16,128]{2,0,1:T(4,128)}), f32[3,16,128]{2,0,1:T(4,128)}, u32[]{:S(2)}, u32[]{:S(2)}) async-start(f32[3,16,128]{2,0,1:T(4,128)} %bitcast.434), calls=%async_computation.6 | async-start | bytes 65536 | tf_op jit(solution)/shard_map/all_to_all | solution.py:63
  531.5 12.0 %scatter_custom_fusion.7 = f32[16384]{0:T(1024)} fusion(s32[2048]{0:T(1024)} %bitcast.458, f32[2048]{0:T(1024)S(1)} %bitcast.443, f32[]{:T(128)} %constant.81.clone.1), kind=kCustom, calls=%fused_computation.688 | custom fusion | flops 2048 | bytes 66048 | tf_op jit(solution)/shard_map/scatter-add | solution.py:74
  559.8 5.7 copy.187
  565.5 11.0 %gather_fusion.16 = f32[2048,3]{1,0:T(8,128)} fusion(f32[3,16384]{0,1:T(8,128)} %bitcast.387, s32[2048]{0:T(1024)S(1)} %fusion.262), kind=kCustom, calls=%fused_computation.16 | custom fusion | bytes 57344 | tf_op jit(solution)/shard_map/gather | solution.py:68
  578.6 11.4 %all-to-all-start.7 = ((f32[3,16,128]{2,0,1:T(4,128)}), f32[3,16,128]{2,0,1:T(4,128)}, u32[]{:S(2)}, u32[]{:S(2)}) async-start(f32[3,16,128]{2,0,1:T(4,128)} %bitcast.113), calls=%async_computation.7 | async-start | bytes 65536 | tf_op jit(solution)/shard_map/all_to_all | solution.py:63
  598.2 11.4 %scatter_custom_fusion.8 = f32[16384]{0:T(1024)S(1)} fusion(s32[2048]{0:T(1024)} %bitcast.459, f32[2048]{0:T(1024)S(1)} %bitcast.450, f32[]{:T(128)} %constant.81.clone.1), kind=kCustom, calls=%fused_computation.686 | custom fusion | flops 2048 | bytes 66048 | tf_op jit(solution)/shard_map/scatter-add | solution.py:74
  654.1 10.9 %gather_fusion.17 = f32[2048,3]{1,0:T(8,128)} fusion(f32[3,16384]{0,1:T(8,128)} %bitcast.388, s32[2048]{0:T(1024)S(1)} %fusion.262), kind=kCustom, calls=%fused_computation.17 | custom fusion | bytes 57344 | tf_op jit(solution)/shard_map/gather | solution.py:68
  667.2 10.7 %all-to-all-start.8 = ((f32[3,16,128]{2,0,1:T(4,128)}), f32[3,16,128]{2,0,1:T(4,128)}, u32[]{:S(2)}, u32[]{:S(2)}) async-start(f32[3,16,128]{2,0,1:T(4,128)} %bitcast.439), calls=%async_computation.8 | async-start | bytes 65536 | tf_op jit(solution)/shard_map/all_to_all | solution.py:63
  685.9 11.4 %scatter_custom_fusion.9 = f32[16384]{0:T(1024)S(1)} fusion(s32[2048]{0:T(1024)} %bitcast.460, f32[2048]{0:T(1024)S(1)} %bitcast.451, f32[]{:T(128)} %constant.81.clone.1), kind=kCustom, calls=%fused_computation.684 | custom fusion | flops 2048 | bytes 66048 | tf_op jit(solution)/shard_map/scatter-add | solution.py:74
  714.1 7.1 collective-permute-start.71
  725.9 10.9 %gather_fusion.18 = f32[2048,3]{1,0:T(8,128)} fusion(f32[3,16384]{0,1:T(8,128)} %bitcast.389, s32[2048]{0:T(1024)S(1)} %fusion.262), kind=kCustom, calls=%fused_computation.18 | custom fusion | bytes 57344 | tf_op jit(solution)/shard_map/gather | solution.py:68
  738.9 7.9 all-to-all-start.9
  755.7 12.0 %scatter_custom_fusion.10 = f32[16384]{0:T(1024)} fusion(s32[2048]{0:T(1024)} %bitcast.461, f32[2048]{0:T(1024)S(1)} %bitcast.452, f32[]{:T(128)} %constant.81.clone.1), kind=kCustom, calls=%fused_computation.682 | custom fusion | flops 2048 | bytes 66048 | tf_op jit(solution)/shard_map/scatter-add | solution.py:74
  787.0 5.7 copy.190
  792.7 10.9 %gather_fusion.19 = f32[2048,3]{1,0:T(8,128)} fusion(f32[3,16384]{0,1:T(8,128)} %bitcast.382, s32[2048]{0:T(1024)S(1)} %fusion.262), kind=kCustom, calls=%fused_computation.19 | custom fusion | bytes 57344 | tf_op jit(solution)/shard_map/gather | solution.py:68
  805.8 11.2 %all-to-all-start.10 = ((f32[3,16,128]{2,0,1:T(4,128)}), f32[3,16,128]{2,0,1:T(4,128)S(1)}, u32[]{:S(2)}, u32[]{:S(2)}) async-start(f32[3,16,128]{2,0,1:T(4,128)} %bitcast.131), calls=%async_computation.10 | async-start | bytes 65536 | tf_op jit(solution)/shard_map/all_to_all | solution.py:63
  825.3 11.4 %scatter_custom_fusion.11 = f32[16384]{0:T(1024)S(1)} fusion(s32[2048]{0:T(1024)} %bitcast.462, f32[2048]{0:T(1024)S(1)} %bitcast.445, f32[]{:T(128)} %constant.81.clone.1), kind=kCustom, calls=%fused_computation.680 | custom fusion | flops 2048 | bytes 66048 | tf_op jit(solution)/shard_map/scatter-add | solution.py:74
  860.2 9.6 add_reduce_fusion
  871.8 7.1 collective-permute-start.77
  889.7 141.0 %reduce-scatter.2.cloned.1.call-done = f32[2,32]{0,1:T(8,128)} async-done(((f32[2,1024]{0,1:T(8,128)}), f32[2,32]{0,1:T(8,128)}) %reduce-scatter.2.cloned.1.call-update) | async-done | bytes 272 | tf_op jit(solution)/shard_map/reduce_scatter | solution.py:282
  (705 shorter events, 439.3 us)
Async XLA Ops:
  53.6 55.2 %all-to-all-start.1 = ((f32[3,16,128]{2,0,1:T(4,128)}), f32[3,16,128]{2,0,1:T(4,128)S(1)}, u32[]{:S(2)}, u32[]{:S(2)}) async-start(f32[3,16,128]{2,0,1:T(4,128)} %bitcast.61), calls=%async_computation.1 | async-start | bytes 65536 | tf_op jit(solution)/shard_map/all_to_all | solution.py:63
  58.7 44.7 %collective-permute-start = (f32[10,1,8,128]{3,2,1,0:T(8,128)S(1)}, f32[10,1,8,128]{3,2,1,0:T(8,128)S(1)}, u32[]{:S(2)}, u32[]{:S(2)}) collective-permute-start(f32[10,1,8,128]{3,2,1,0:T(8,128)S(1)} %get-tuple-element.154), channel_id=1, source_target_pairs={{0,16},{1,17},{2,18},{3,19},{4,20},{5,21},{6,22},{7,23},{8,24},{9,... | collective-permute-start | bytes 122888 | tf_op jit(solution)/shard_map/ppermute | solution.py:18
  62.1 41.3 %collective-permute-start.1 = (f32[10,1,8,128]{3,2,1,0:T(8,128)S(1)}, f32[10,1,8,128]{3,2,1,0:T(8,128)S(1)}, u32[]{:S(2)}, u32[]{:S(2)}) collective-permute-start(f32[10,1,8,128]{3,2,1,0:T(8,128)S(1)} %get-tuple-element.155), channel_id=1, source_target_pairs={{16,0},{17,1},{18,2},{19,3},{20,4},{21,5},{22,6},{23,7},{24,8},{25... | collective-permute-start | bytes 122888 | tf_op jit(solution)/shard_map/ppermute | solution.py:21
  71.3 25.7 %collective-permute-start.6 = (f32[3,18,1,128]{3,2,1,0:T(1,128)}, f32[3,18,1,128]{3,2,1,0:T(1,128)S(1)}, u32[]{:S(2)}, u32[]{:S(2)}) collective-permute-start(f32[3,18,1,128]{3,2,1,0:T(1,128)} %get-tuple-element.227), channel_id=1, source_target_pairs={{4,0},{8,4},{12,8},{5,1},{9,5},{13,9},{6,2},{10,6},{14,10},{7,3},{... | collective-permute-start | bytes 82952 | tf_op jit(solution)/shard_map/ppermute | solution.py:21
  72.6 24.5 %collective-permute-start.7 = (f32[3,18,1,128]{3,2,1,0:T(1,128)}, f32[3,18,1,128]{3,2,1,0:T(1,128)S(1)}, u32[]{:S(2)}, u32[]{:S(2)}) collective-permute-start(f32[3,18,1,128]{3,2,1,0:T(1,128)} %get-tuple-element.226), channel_id=1, source_target_pairs={{0,4},{4,8},{8,12},{1,5},{5,9},{9,13},{2,6},{6,10},{10,14},{3,7},{... | collective-permute-start | bytes 82952 | tf_op jit(solution)/shard_map/ppermute | solution.py:18
  98.1 59.0 %collective-permute-start.10 = (f32[3,18,10,1]{3,2,1,0:T(8,128)}, f32[3,18,10,1]{3,2,1,0:T(8,128)}, u32[]{:S(2)}, u32[]{:S(2)}) collective-permute-start(f32[3,18,10,1]{3,2,1,0:T(8,128)} %get-tuple-element.179), channel_id=1, source_target_pairs={{1,0},{2,1},{3,2},{5,4},{6,5},{7,6},{9,8},{10,9},{11,10},{13,12},{... | collective-permute-start | bytes 6488 | tf_op jit(solution)/shard_map/ppermute | solution.py:21
  99.6 57.6 %collective-permute-start.11 = (f32[3,18,10,1]{3,2,1,0:T(8,128)}, f32[3,18,10,1]{3,2,1,0:T(8,128)}, u32[]{:S(2)}, u32[]{:S(2)}) collective-permute-start(f32[3,18,10,1]{3,2,1,0:T(8,128)} %get-tuple-element.178), channel_id=1, source_target_pairs={{0,1},{1,2},{2,3},{4,5},{5,6},{6,7},{8,9},{9,10},{10,11},{12,13},{... | collective-permute-start | bytes 6488 | tf_op jit(solution)/shard_map/ppermute | solution.py:18
  103.5 31.5 %collective-permute-start.4 = (f32[10,18,1,128]{3,2,1,0:T(1,128)S(1)}, f32[10,18,1,128]{3,2,1,0:T(1,128)S(1)}, u32[]{:S(2)}, u32[]{:S(2)}) collective-permute-start(f32[10,18,1,128]{3,2,1,0:T(1,128)S(1)} %get-tuple-element.152), channel_id=1, source_target_pairs={{0,4},{4,8},{8,12},{1,5},{5,9},{9,13},{2,6},{6,10},{10,14},{3,7},{... | collective-permute-start | bytes 276488 | tf_op jit(solution)/shard_map/ppermute | solution.py:18
  107.4 27.8 %collective-permute-start.5 = (f32[10,18,1,128]{3,2,1,0:T(1,128)S(1)}, f32[10,18,1,128]{3,2,1,0:T(1,128)S(1)}, u32[]{:S(2)}, u32[]{:S(2)}) collective-permute-start(f32[10,18,1,128]{3,2,1,0:T(1,128)S(1)} %get-tuple-element.153), channel_id=1, source_target_pairs={{4,0},{8,4},{12,8},{5,1},{9,5},{13,9},{6,2},{10,6},{14,10},{7,3},{... | collective-permute-start | bytes 276488 | tf_op jit(solution)/shard_map/ppermute | solution.py:21
  168.3 29.4 %collective-permute-start.14 = (f32[3,18,1,128]{3,2,1,0:T(1,128)}, f32[3,18,1,128]{3,2,1,0:T(1,128)}, u32[]{:S(2)}, u32[]{:S(2)}) collective-permute-start(f32[3,18,1,128]{3,2,1,0:T(1,128)} %get-tuple-element.225), channel_id=1, source_target_pairs={{4,0},{8,4},{12,8},{5,1},{9,5},{13,9},{6,2},{10,6},{14,10},{7,3},{... | collective-permute-start | bytes 82952 | tf_op jit(solution)/shard_map/ppermute | solution.py:21
  169.6 28.1 %collective-permute-start.15 = (f32[3,18,1,128]{3,2,1,0:T(1,128)}, f32[3,18,1,128]{3,2,1,0:T(1,128)}, u32[]{:S(2)}, u32[]{:S(2)}) collective-permute-start(f32[3,18,1,128]{3,2,1,0:T(1,128)} %get-tuple-element.224), channel_id=1, source_target_pairs={{0,4},{4,8},{8,12},{1,5},{5,9},{9,13},{2,6},{6,10},{10,14},{3,7},{... | collective-permute-start | bytes 82952 | tf_op jit(solution)/shard_map/ppermute | solution.py:18
  229.5 36.4 %collective-permute-start.20 = (f32[3,18,1,128]{3,2,1,0:T(1,128)}, f32[3,18,1,128]{3,2,1,0:T(1,128)}, u32[]{:S(2)}, u32[]{:S(2)}) collective-permute-start(f32[3,18,1,128]{3,2,1,0:T(1,128)} %get-tuple-element.223), channel_id=1, source_target_pairs={{4,0},{8,4},{12,8},{5,1},{9,5},{13,9},{6,2},{10,6},{14,10},{7,3},{... | collective-permute-start | bytes 82952 | tf_op jit(solution)/shard_map/ppermute | solution.py:21
  230.8 35.1 %collective-permute-start.21 = (f32[3,18,1,128]{3,2,1,0:T(1,128)}, f32[3,18,1,128]{3,2,1,0:T(1,128)}, u32[]{:S(2)}, u32[]{:S(2)}) collective-permute-start(f32[3,18,1,128]{3,2,1,0:T(1,128)} %get-tuple-element.222), channel_id=1, source_target_pairs={{0,4},{4,8},{8,12},{1,5},{5,9},{9,13},{2,6},{6,10},{10,14},{3,7},{... | collective-permute-start | bytes 82952 | tf_op jit(solution)/shard_map/ppermute | solution.py:18
  254.7 20.1 %all-to-all-start.3 = ((f32[3,16,128]{2,0,1:T(4,128)}), f32[3,16,128]{2,0,1:T(4,128)}, u32[]{:S(2)}, u32[]{:S(2)}) async-start(f32[3,16,128]{2,0,1:T(4,128)} %bitcast.436), calls=%async_computation.3 | async-start | bytes 65536 | tf_op jit(solution)/shard_map/all_to_all | solution.py:63
  297.7 36.6 %collective-permute-start.26 = (f32[3,18,1,128]{3,2,1,0:T(1,128)}, f32[3,18,1,128]{3,2,1,0:T(1,128)}, u32[]{:S(2)}, u32[]{:S(2)}) collective-permute-start(f32[3,18,1,128]{3,2,1,0:T(1,128)} %get-tuple-element.221), channel_id=1, source_target_pairs={{4,0},{8,4},{12,8},{5,1},{9,5},{13,9},{6,2},{10,6},{14,10},{7,3},{... | collective-permute-start | bytes 82952 | tf_op jit(solution)/shard_map/ppermute | solution.py:21
  299.0 35.4 %collective-permute-start.27 = (f32[3,18,1,128]{3,2,1,0:T(1,128)}, f32[3,18,1,128]{3,2,1,0:T(1,128)}, u32[]{:S(2)}, u32[]{:S(2)}) collective-permute-start(f32[3,18,1,128]{3,2,1,0:T(1,128)} %get-tuple-element.220), channel_id=1, source_target_pairs={{0,4},{4,8},{8,12},{1,5},{5,9},{9,13},{2,6},{6,10},{10,14},{3,7},{... | collective-permute-start | bytes 82952 | tf_op jit(solution)/shard_map/ppermute | solution.py:18
  323.1 20.2 %all-to-all-start.4 = ((f32[3,16,128]{2,0,1:T(4,128)}), f32[3,16,128]{2,0,1:T(4,128)}, u32[]{:S(2)}, u32[]{:S(2)}) async-start(f32[3,16,128]{2,0,1:T(4,128)} %bitcast.437), calls=%async_computation.4 | async-start | bytes 65536 | tf_op jit(solution)/shard_map/all_to_all | solution.py:63
  366.3 72.9 %collective-permute-start.32 = (f32[3,18,1,128]{3,2,1,0:T(1,128)}, f32[3,18,1,128]{3,2,1,0:T(1,128)}, u32[]{:S(2)}, u32[]{:S(2)}) collective-permute-start(f32[3,18,1,128]{3,2,1,0:T(1,128)} %get-tuple-element.219), channel_id=1, source_target_pairs={{4,0},{8,4},{12,8},{5,1},{9,5},{13,9},{6,2},{10,6},{14,10},{7,3},{... | collective-permute-start | bytes 82952 | tf_op jit(solution)/shard_map/ppermute | solution.py:21
  367.6 71.6 %collective-permute-start.33 = (f32[3,18,1,128]{3,2,1,0:T(1,128)}, f32[3,18,1,128]{3,2,1,0:T(1,128)}, u32[]{:S(2)}, u32[]{:S(2)}) collective-permute-start(f32[3,18,1,128]{3,2,1,0:T(1,128)} %get-tuple-element.218), channel_id=1, source_target_pairs={{0,4},{4,8},{8,12},{1,5},{5,9},{9,13},{2,6},{6,10},{10,14},{3,7},{... | collective-permute-start | bytes 82952 | tf_op jit(solution)/shard_map/ppermute | solution.py:18
  428.0 20.1 %all-to-all-start.5 = ((f32[3,16,128]{2,0,1:T(4,128)}), f32[3,16,128]{2,0,1:T(4,128)}, u32[]{:S(2)}, u32[]{:S(2)}) async-start(f32[3,16,128]{2,0,1:T(4,128)} %bitcast.438), calls=%async_computation.5 | async-start | bytes 65536 | tf_op jit(solution)/shard_map/all_to_all | solution.py:63
  481.8 39.2 %collective-permute-start.38 = (f32[3,18,1,128]{3,2,1,0:T(1,128)}, f32[3,18,1,128]{3,2,1,0:T(1,128)}, u32[]{:S(2)}, u32[]{:S(2)}) collective-permute-start(f32[3,18,1,128]{3,2,1,0:T(1,128)} %get-tuple-element.217), channel_id=1, source_target_pairs={{4,0},{8,4},{12,8},{5,1},{9,5},{13,9},{6,2},{10,6},{14,10},{7,3},{... | collective-permute-start | bytes 82952 | tf_op jit(solution)/shard_map/ppermute | solution.py:21
  483.1 37.9 %collective-permute-start.39 = (f32[3,18,1,128]{3,2,1,0:T(1,128)}, f32[3,18,1,128]{3,2,1,0:T(1,128)}, u32[]{:S(2)}, u32[]{:S(2)}) collective-permute-start(f32[3,18,1,128]{3,2,1,0:T(1,128)} %get-tuple-element.216), channel_id=1, source_target_pairs={{0,4},{4,8},{8,12},{1,5},{5,9},{9,13},{2,6},{6,10},{10,14},{3,7},{... | collective-permute-start | bytes 82952 | tf_op jit(solution)/shard_map/ppermute | solution.py:18
  509.8 20.2 %all-to-all-start.6 = ((f32[3,16,128]{2,0,1:T(4,128)}), f32[3,16,128]{2,0,1:T(4,128)}, u32[]{:S(2)}, u32[]{:S(2)}) async-start(f32[3,16,128]{2,0,1:T(4,128)} %bitcast.434), calls=%async_computation.6 | async-start | bytes 65536 | tf_op jit(solution)/shard_map/all_to_all | solution.py:63
  553.2 36.8 %collective-permute-start.44 = (f32[3,18,1,128]{3,2,1,0:T(1,128)S(1)}, f32[3,18,1,128]{3,2,1,0:T(1,128)S(1)}, u32[]{:S(2)}, u32[]{:S(2)}) collective-permute-start(f32[3,18,1,128]{3,2,1,0:T(1,128)S(1)} %get-tuple-element.215), channel_id=1, source_target_pairs={{4,0},{8,4},{12,8},{5,1},{9,5},{13,9},{6,2},{10,6},{14,10},{7,3},{... | collective-permute-start | bytes 82952 | tf_op jit(solution)/shard_map/ppermute | solution.py:21
  554.5 35.5 %collective-permute-start.45 = (f32[3,18,1,128]{3,2,1,0:T(1,128)S(1)}, f32[3,18,1,128]{3,2,1,0:T(1,128)S(1)}, u32[]{:S(2)}, u32[]{:S(2)}) collective-permute-start(f32[3,18,1,128]{3,2,1,0:T(1,128)S(1)} %get-tuple-element.214), channel_id=1, source_target_pairs={{0,4},{4,8},{8,12},{1,5},{5,9},{9,13},{2,6},{6,10},{10,14},{3,7},{... | collective-permute-start | bytes 82952 | tf_op jit(solution)/shard_map/ppermute | solution.py:18
  578.6 18.8 %all-to-all-start.7 = ((f32[3,16,128]{2,0,1:T(4,128)}), f32[3,16,128]{2,0,1:T(4,128)}, u32[]{:S(2)}, u32[]{:S(2)}) async-start(f32[3,16,128]{2,0,1:T(4,128)} %bitcast.113), calls=%async_computation.7 | async-start | bytes 65536 | tf_op jit(solution)/shard_map/all_to_all | solution.py:63
  611.5 24.3 %collective-permute-start.48 = (f32[3,1,8,128]{3,2,1,0:T(8,128)}, f32[3,1,8,128]{3,2,1,0:T(8,128)S(1)}, u32[]{:S(2)}, u32[]{:S(2)}) collective-permute-start(f32[3,1,8,128]{3,2,1,0:T(8,128)} %get-tuple-element.243), channel_id=1, source_target_pairs={{16,0},{17,1},{18,2},{19,3},{20,4},{21,5},{22,6},{23,7},{24,8},{25... | collective-permute-start | bytes 36872 | tf_op jit(solution)/shard_map/ppermute | solution.py:21
  612.8 23.0 %collective-permute-start.49 = (f32[3,1,8,128]{3,2,1,0:T(8,128)S(1)}, f32[3,1,8,128]{3,2,1,0:T(8,128)S(1)}, u32[]{:S(2)}, u32[]{:S(2)}) collective-permute-start(f32[3,1,8,128]{3,2,1,0:T(8,128)S(1)} %get-tuple-element.242), channel_id=1, source_target_pairs={{0,16},{1,17},{2,18},{3,19},{4,20},{5,21},{6,22},{7,23},{8,24},{9,... | collective-permute-start | bytes 36872 | tf_op jit(solution)/shard_map/ppermute | solution.py:18
  617.4 24.9 %collective-permute-start.66 = (f32[3,1,8,128]{3,2,1,0:T(8,128)S(1)}, f32[3,1,8,128]{3,2,1,0:T(8,128)S(1)}, u32[]{:S(2)}, u32[]{:S(2)}) collective-permute-start(f32[3,1,8,128]{3,2,1,0:T(8,128)S(1)} %get-tuple-element.229), channel_id=1, source_target_pairs={{16,0},{17,1},{18,2},{19,3},{20,4},{21,5},{22,6},{23,7},{24,8},{25... | collective-permute-start | bytes 36872 | tf_op jit(solution)/shard_map/ppermute | solution.py:21
  618.7 23.7 %collective-permute-start.67 = (f32[3,1,8,128]{3,2,1,0:T(8,128)S(1)}, f32[3,1,8,128]{3,2,1,0:T(8,128)S(1)}, u32[]{:S(2)}, u32[]{:S(2)}) collective-permute-start(f32[3,1,8,128]{3,2,1,0:T(8,128)S(1)} %get-tuple-element.228), channel_id=1, source_target_pairs={{0,16},{1,17},{2,18},{3,19},{4,20},{5,21},{6,22},{7,23},{8,24},{9,... | collective-permute-start | bytes 36872 | tf_op jit(solution)/shard_map/ppermute | solution.py:18
  636.5 41.3 %collective-permute-start.50 = (f32[3,18,1,128]{3,2,1,0:T(1,128)}, f32[3,18,1,128]{3,2,1,0:T(1,128)S(1)}, u32[]{:S(2)}, u32[]{:S(2)}) collective-permute-start(f32[3,18,1,128]{3,2,1,0:T(1,128)} %get-tuple-element.213), channel_id=1, source_target_pairs={{4,0},{8,4},{12,8},{5,1},{9,5},{13,9},{6,2},{10,6},{14,10},{7,3},{... | collective-permute-start | bytes 82952 | tf_op jit(solution)/shard_map/ppermute | solution.py:21
  637.8 40.1 %collective-permute-start.51 = (f32[3,18,1,128]{3,2,1,0:T(1,128)}, f32[3,18,1,128]{3,2,1,0:T(1,128)S(1)}, u32[]{:S(2)}, u32[]{:S(2)}) collective-permute-start(f32[3,18,1,128]{3,2,1,0:T(1,128)} %get-tuple-element.212), channel_id=1, source_target_pairs={{0,4},{4,8},{8,12},{1,5},{5,9},{9,13},{2,6},{6,10},{10,14},{3,7},{... | collective-permute-start | bytes 82952 | tf_op jit(solution)/shard_map/ppermute | solution.py:18
  643.0 61.4 %collective-permute-start.68 = (f32[3,18,1,128]{3,2,1,0:T(1,128)}, f32[3,18,1,128]{3,2,1,0:T(1,128)S(1)}, u32[]{:S(2)}, u32[]{:S(2)}) collective-permute-start(f32[3,18,1,128]{3,2,1,0:T(1,128)} %get-tuple-element.201), channel_id=1, source_target_pairs={{4,0},{8,4},{12,8},{5,1},{9,5},{13,9},{6,2},{10,6},{14,10},{7,3},{... | collective-permute-start | bytes 82952 | tf_op jit(solution)/shard_map/ppermute | solution.py:21
  644.3 60.2 %collective-permute-start.69 = (f32[3,18,1,128]{3,2,1,0:T(1,128)}, f32[3,18,1,128]{3,2,1,0:T(1,128)}, u32[]{:S(2)}, u32[]{:S(2)}) collective-permute-start(f32[3,18,1,128]{3,2,1,0:T(1,128)} %get-tuple-element.200), channel_id=1, source_target_pairs={{0,4},{4,8},{8,12},{1,5},{5,9},{9,13},{2,6},{6,10},{10,14},{3,7},{... | collective-permute-start | bytes 82952 | tf_op jit(solution)/shard_map/ppermute | solution.py:18
  667.2 18.0 %all-to-all-start.8 = ((f32[3,16,128]{2,0,1:T(4,128)}), f32[3,16,128]{2,0,1:T(4,128)}, u32[]{:S(2)}, u32[]{:S(2)}) async-start(f32[3,16,128]{2,0,1:T(4,128)} %bitcast.439), calls=%async_computation.8 | async-start | bytes 65536 | tf_op jit(solution)/shard_map/all_to_all | solution.py:63
  705.9 41.0 %collective-permute-start.56 = (f32[3,18,1,128]{3,2,1,0:T(1,128)S(1)}, f32[3,18,1,128]{3,2,1,0:T(1,128)S(1)}, u32[]{:S(2)}, u32[]{:S(2)}) collective-permute-start(f32[3,18,1,128]{3,2,1,0:T(1,128)S(1)} %get-tuple-element.211), channel_id=1, source_target_pairs={{4,0},{8,4},{12,8},{5,1},{9,5},{13,9},{6,2},{10,6},{14,10},{7,3},{... | collective-permute-start | bytes 82952 | tf_op jit(solution)/shard_map/ppermute | solution.py:21
  707.2 39.7 %collective-permute-start.57 = (f32[3,18,1,128]{3,2,1,0:T(1,128)S(1)}, f32[3,18,1,128]{3,2,1,0:T(1,128)S(1)}, u32[]{:S(2)}, u32[]{:S(2)}) collective-permute-start(f32[3,18,1,128]{3,2,1,0:T(1,128)S(1)} %get-tuple-element.210), channel_id=1, source_target_pairs={{0,4},{4,8},{8,12},{1,5},{5,9},{9,13},{2,6},{6,10},{10,14},{3,7},{... | collective-permute-start | bytes 82952 | tf_op jit(solution)/shard_map/ppermute | solution.py:18
  712.8 72.0 %collective-permute-start.70 = (f32[3,18,10,1]{3,2,1,0:T(8,128)}, f32[3,18,10,1]{3,2,1,0:T(8,128)}, u32[]{:S(2)}, u32[]{:S(2)}) collective-permute-start(f32[3,18,10,1]{3,2,1,0:T(8,128)} %get-tuple-element.157), channel_id=1, source_target_pairs={{1,0},{2,1},{3,2},{5,4},{6,5},{7,6},{9,8},{10,9},{11,10},{13,12},{... | collective-permute-start | bytes 6488 | tf_op jit(solution)/shard_map/ppermute | solution.py:21
  714.1 70.7 %collective-permute-start.71 = (f32[3,18,10,1]{3,2,1,0:T(8,128)}, f32[3,18,10,1]{3,2,1,0:T(8,128)}, u32[]{:S(2)}, u32[]{:S(2)}) collective-permute-start(f32[3,18,10,1]{3,2,1,0:T(8,128)} %get-tuple-element.156), channel_id=1, source_target_pairs={{0,1},{1,2},{2,3},{4,5},{5,6},{6,7},{8,9},{9,10},{10,11},{12,13},{... | collective-permute-start | bytes 6488 | tf_op jit(solution)/shard_map/ppermute | solution.py:18
  738.9 15.9 %all-to-all-start.9 = ((f32[3,16,128]{2,0,1:T(4,128)}), f32[3,16,128]{2,0,1:T(4,128)}, u32[]{:S(2)}, u32[]{:S(2)}) async-start(f32[3,16,128]{2,0,1:T(4,128)} %bitcast.125), calls=%async_computation.9 | async-start | bytes 65536 | tf_op jit(solution)/shard_map/all_to_all | solution.py:63
  778.2 38.8 %collective-permute-start.62 = (f32[3,18,1,128]{3,2,1,0:T(1,128)}, f32[3,18,1,128]{3,2,1,0:T(1,128)}, u32[]{:S(2)}, u32[]{:S(2)}) collective-permute-start(f32[3,18,1,128]{3,2,1,0:T(1,128)} %get-tuple-element.209), channel_id=1, source_target_pairs={{4,0},{8,4},{12,8},{5,1},{9,5},{13,9},{6,2},{10,6},{14,10},{7,3},{... | collective-permute-start | bytes 82952 | tf_op jit(solution)/shard_map/ppermute | solution.py:21
  779.7 37.4 %collective-permute-start.63 = (f32[3,18,1,128]{3,2,1,0:T(1,128)}, f32[3,18,1,128]{3,2,1,0:T(1,128)}, u32[]{:S(2)}, u32[]{:S(2)}) collective-permute-start(f32[3,18,1,128]{3,2,1,0:T(1,128)} %get-tuple-element.208), channel_id=1, source_target_pairs={{0,4},{4,8},{8,12},{1,5},{5,9},{9,13},{2,6},{6,10},{10,14},{3,7},{... | collective-permute-start | bytes 82952 | tf_op jit(solution)/shard_map/ppermute | solution.py:18
  805.8 19.4 %all-to-all-start.10 = ((f32[3,16,128]{2,0,1:T(4,128)}), f32[3,16,128]{2,0,1:T(4,128)S(1)}, u32[]{:S(2)}, u32[]{:S(2)}) async-start(f32[3,16,128]{2,0,1:T(4,128)} %bitcast.131), calls=%async_computation.10 | async-start | bytes 65536 | tf_op jit(solution)/shard_map/all_to_all | solution.py:63
  817.0 213.6 %reduce-scatter.2.cloned.1.call-start = ((), (), s32[]{:S(2)}) async-start(), calls=%async_computation.12 | async-start | bytes 540672 | tf_op jit(solution)/shard_map/reduce_scatter | solution.py:282
  838.0 16.3 %collective-permute-start.72 = (f32[3,1,8,128]{3,2,1,0:T(8,128)S(1)}, f32[3,1,8,128]{3,2,1,0:T(8,128)S(1)}, u32[]{:S(2)}, u32[]{:S(2)}) collective-permute-start(f32[3,1,8,128]{3,2,1,0:T(8,128)S(1)} %get-tuple-element.231), channel_id=1, source_target_pairs={{16,0},{17,1},{18,2},{19,3},{20,4},{21,5},{22,6},{23,7},{24,8},{25... | collective-permute-start | bytes 36872 | tf_op jit(solution)/shard_map/ppermute | solution.py:21
  839.3 15.0 %collective-permute-start.73 = (f32[3,1,8,128]{3,2,1,0:T(8,128)S(1)}, f32[3,1,8,128]{3,2,1,0:T(8,128)S(1)}, u32[]{:S(2)}, u32[]{:S(2)}) collective-permute-start(f32[3,1,8,128]{3,2,1,0:T(8,128)S(1)} %get-tuple-element.230), channel_id=1, source_target_pairs={{0,16},{1,17},{2,18},{3,19},{4,20},{5,21},{6,22},{7,23},{8,24},{9,... | collective-permute-start | bytes 36872 | tf_op jit(solution)/shard_map/ppermute | solution.py:18
  854.3 15.6 %collective-permute-start.74 = (f32[3,18,1,128]{3,2,1,0:T(1,128)S(1)}, f32[3,18,1,128]{3,2,1,0:T(1,128)S(1)}, u32[]{:S(2)}, u32[]{:S(2)}) collective-permute-start(f32[3,18,1,128]{3,2,1,0:T(1,128)S(1)} %get-tuple-element.207), channel_id=1, source_target_pairs={{4,0},{8,4},{12,8},{5,1},{9,5},{13,9},{6,2},{10,6},{14,10},{7,3},{... | collective-permute-start | bytes 82952 | tf_op jit(solution)/shard_map/ppermute | solution.py:21
  855.6 14.3 %collective-permute-start.75 = (f32[3,18,1,128]{3,2,1,0:T(1,128)S(1)}, f32[3,18,1,128]{3,2,1,0:T(1,128)S(1)}, u32[]{:S(2)}, u32[]{:S(2)}) collective-permute-start(f32[3,18,1,128]{3,2,1,0:T(1,128)S(1)} %get-tuple-element.206), channel_id=1, source_target_pairs={{0,4},{4,8},{8,12},{1,5},{5,9},{9,13},{2,6},{6,10},{10,14},{3,7},{... | collective-permute-start | bytes 82952 | tf_op jit(solution)/shard_map/ppermute | solution.py:18
  (185 other events, 2012.6 us)
Sparse Core Ops, SparseCore 0:
  889.0 141.5 reduce-scatter.1
where the time goes:
time: 1060 us; the launch traced here: 1040 us
  starting transfers between devices  321 us (30%)
  local copies, waits for them, and re-layouts  285 us (27%)
  other arithmetic  245 us (23%)
  waiting for transfers between devices  161 us (15%)
  between operations  17.7 us (2%)
    ppermute x39, starting transfers between devices, extended_2(): lax.ppermute(lax.slice_in_dim(block, block.shape[dim] - width, None, axis...  169 us
    reduce_scatter x1, waiting for transfers between devices, local(): lax.psum_scatter(region_partial, ('gx', 'gy', 'gz'), scatter_dimension=1,...  141 us
    gather x20, local copies, waits for them, and re-layouts, fault_sum(): own_values = flattened[:, cell_index]  131 us
    scatter-add x10, other arithmetic, fault_sum(): faults = jnp.zeros((flattened.shape[1],), jnp.float32).at[cell_index.resh...  118 us
    all_to_all x10, starting transfers between devices, fault_exchange(): lax.all_to_all(values, ('gy', 'gz'), split_axis=1, concat_axis=1, tiled=T...  94.9 us
    reshape x10, local copies, waits for them, and re-layouts, fault_sum(): flattened = lagrange.reshape(lagrange.shape[0], -1)  53.4 us
    ppermute x39, starting transfers between devices, extended_2(): lax.ppermute(lax.slice_in_dim(block, 0, width, axis=dim), axis, backward)  51.4 us
  transfers between devices with their start and end apart: 90, of which 19 were waited for; matrix products, arithmetic and copies ran while one was open for 35% of the time, Pallas kernels for 0%

commit v1 on v0

--- a/solution.py
+++ b/solution.py
@@ -8,6 +8,12 @@
 PARAM_REGIONS = 32
 fluid_viscosity = (0.4, 0.5, 1.0)
 sigma_sq = 64.0
+move_edges_up = lambda vec: jnp.concatenate(
+    lax.all_to_all(
+        jnp.stack(jnp.split(vec, lax.axis_size(("gy", "gz")), axis=1), axis=0), ("gy", "gz"), 0, 0
+    ),
+    axis=1,
+)
 
 
 def extended_2(block, sides, width):
@@ -60,7 +66,7 @@
 
 
 def fault_exchange(values):
-    return lax.all_to_all(values, ("gy", "gz"), split_axis=1, concat_axis=1, tiled=True)
+    return move_edges_up(values)
 
 
 def fault_sum(lagrange, coefficient, cell_index):

time: 1060 us -> 1080 us (1.019)
  local copies, waits for them, and re-layouts: 285 us -> 358 us
  other arithmetic: 245 us -> 203 us
    unnamed x288 -> x378, local copies, waits for them, and re-layouts: 4.35 us -> 90.8 us
  transfers between devices with their start and end apart: 90 -> 90, of which waited for: 19 -> 21; matrix products, arithmetic and copies ran while one was open for 35% -> 15% of each run, Pallas kernels for 0% -> 0%
where the time goes in v1:
time: 1080 us; the launch traced here: 1070 us
  local copies, waits for them, and re-layouts  358 us (33%)
  starting transfers between devices  317 us (29%)
  other arithmetic  203 us (19%)
  waiting for transfers between devices  165 us (15%)
  between operations  17.6 us (2%)
    ppermute x39, starting transfers between devices, extended_2(): lax.ppermute(lax.slice_in_dim(block, block.shape[dim] - width, None, axis...  160 us
    reduce_scatter x1, waiting for transfers between devices, local(): lax.psum_scatter(region_partial, ('gx', 'gy', 'gz'), scatter_dimension=1,...  141 us
    gather x20, local copies, waits for them, and re-layouts, fault_sum(): own_values = flattened[:, cell_index]  125 us
    scatter-add x10, other arithmetic, fault_sum(): faults = jnp.zeros((flattened.shape[1],), jnp.float32).at[cell_index.resh...  115 us
    all_to_all x10, starting transfers between devices, lax.all_to_all(jnp.stack(jnp.split(vec, lax.axis_size(('gy', 'gz')), axis...  100 us
    unnamed x378, local copies, waits for them, and re-layouts  90.8 us
    ppermute x39, starting transfers between devices, extended_2(): lax.ppermute(lax.slice_in_dim(block, 0, width, axis=dim), axis, backward)  51.1 us
    reshape x10, local copies, waits for them, and re-layouts, fault_sum(): flattened = lagrange.reshape(lagrange.shape[0], -1)  47.4 us
  transfers between devices with their start and end apart: 90, of which 21 were waited for; matrix products, arithmetic and copies ran while one was open for 15% of the time, Pallas kernels for 0%

profile of v1, /device:TPU:0, one launch (start us, length us, event | category | flops | bytes accessed | tf_op | source)
XLA Modules:
  0.0 1069.3 jit_solution(17115476830173005751)
XLA Ops:
  18.0 8.5 psum.7
  36.5 4.6 copy.862
  41.2 11.0 %gather_fusion.8 = f32[2048,3]{1,0:T(8,128)} fusion(f32[3,16384]{0,1:T(8,128)} %bitcast.1089, s32[2048]{0:T(1024)S(1)} %fusion.272), kind=kCustom, calls=%fused_computation.8 | custom fusion | bytes 57344 | tf_op jit(solution)/shard_map/gather | solution.py:74
  63.0 5.0 all-to-all-start.1
  81.1 5.0 collective-permute-start.7
  87.5 5.3 copy.813
  92.9 11.0 %gather_fusion.7 = f32[2048,6]{1,0:T(8,128)} fusion(f32[6,16384]{0,1:T(8,128)} %copy.813, s32[2048]{0:T(1024)S(1)} %fusion.272), kind=kCustom, calls=%fused_computation.7 | custom fusion | bytes 106496 | tf_op jit(solution)/shard_map/gather | solution.py:178
  141.0 5.9 all-to-all-start
  146.9 6.8 all-to-all-done
  155.3 12.0 %scatter_custom_fusion.1 = f32[16384]{0:T(1024)} fusion(s32[2048]{0:T(1024)} %bitcast.1299, f32[2048]{0:T(1024)S(1)} %bitcast.1298, f32[]{:T(128)} %constant.81.clone.1), kind=kCustom, calls=%fused_computation.872 | custom fusion | flops 2048 | bytes 66048 | tf_op jit(solution)/shard_map/scatter-add | solution.py:80
  194.1 5.6 copy.863
  201.0 11.0 %gather_fusion.9 = f32[2048,3]{1,0:T(8,128)} fusion(f32[3,16384]{0,1:T(8,128)} %bitcast.1082, s32[2048]{0:T(1024)S(1)} %fusion.272), kind=kCustom, calls=%fused_computation.9 | custom fusion | bytes 57344 | tf_op jit(solution)/shard_map/gather | solution.py:74
  249.2 11.4 %scatter_custom_fusion.2 = f32[16384]{0:T(1024)S(1)} fusion(s32[2048]{0:T(1024)} %bitcast.1300, f32[2048]{0:T(1024)S(1)} %bitcast.1311, f32[]{:T(128)} %constant.81.clone.1), kind=kCustom, calls=%fused_computation.870 | custom fusion | flops 2048 | bytes 66048 | tf_op jit(solution)/shard_map/scatter-add | solution.py:80
  261.9 4.6 copy.864
  266.6 10.9 %gather_fusion.10 = f32[2048,3]{1,0:T(8,128)} fusion(f32[3,16384]{0,1:T(8,128)} %bitcast.1083, s32[2048]{0:T(1024)S(1)} %fusion.272), kind=kCustom, calls=%fused_computation.10 | custom fusion | bytes 57344 | tf_op jit(solution)/shard_map/gather | solution.py:74
  296.3 4.8 collective-permute-start.21
  301.8 11.5 %all-to-all-start.3 = ((f32[16,3,1,128]{3,2,1,0:T(1,128)}), f32[16,3,1,128]{3,2,1,0:T(1,128)}, u32[]{:S(2)}, u32[]{:S(2)}) async-start(f32[16,3,1,128]{3,2,1,0:T(1,128)} %constant_dynamic-update-slice_fusion.41), calls=%async_computation.3 | async-start | bytes 49152 | tf_op jit(solution)/shard_map/all_to_all | solution.py:12
  321.3 11.6 %scatter_custom_fusion.3 = f32[16384]{0:T(1024)S(1)} fusion(s32[2048]{0:T(1024)} %bitcast.1301, f32[2048]{0:T(1024)S(1)} %bitcast.1312, f32[]{:T(128)} %constant.81.clone.1), kind=kCustom, calls=%fused_computation.868 | custom fusion | flops 2048 | bytes 66048 | tf_op jit(solution)/shard_map/scatter-add | solution.py:80
  334.2 4.6 copy.865
  338.8 10.9 %gather_fusion.11 = f32[2048,3]{1,0:T(8,128)} fusion(f32[3,16384]{0,1:T(8,128)} %bitcast.1084, s32[2048]{0:T(1024)S(1)} %fusion.272), kind=kCustom, calls=%fused_computation.11 | custom fusion | bytes 57344 | tf_op jit(solution)/shard_map/gather | solution.py:74
  373.7 11.2 %all-to-all-start.4 = ((f32[16,3,1,128]{3,2,1,0:T(1,128)}), f32[16,3,1,128]{3,2,1,0:T(1,128)}, u32[]{:S(2)}, u32[]{:S(2)}) async-start(f32[16,3,1,128]{3,2,1,0:T(1,128)} %constant_dynamic-update-slice_fusion.57), calls=%async_computation.4 | async-start | bytes 49152 | tf_op jit(solution)/shard_map/all_to_all | solution.py:12
  393.0 11.4 %scatter_custom_fusion.4 = f32[16384]{0:T(1024)S(1)} fusion(s32[2048]{0:T(1024)} %bitcast.1302, f32[2048]{0:T(1024)S(1)} %bitcast.1313, f32[]{:T(128)} %constant.81.clone.1), kind=kCustom, calls=%fused_computation.866 | custom fusion | flops 2048 | bytes 66048 | tf_op jit(solution)/shard_map/scatter-add | solution.py:80
  405.7 4.6 copy.866
  410.3 10.9 %gather_fusion.12 = f32[2048,3]{1,0:T(8,128)} fusion(f32[3,16384]{0,1:T(8,128)} %bitcast.1085, s32[2048]{0:T(1024)S(1)} %fusion.272), kind=kCustom, calls=%fused_computation.12 | custom fusion | bytes 57344 | tf_op jit(solution)/shard_map/gather | solution.py:74
  445.2 11.2 %all-to-all-start.5 = ((f32[16,3,1,128]{3,2,1,0:T(1,128)}), f32[16,3,1,128]{3,2,1,0:T(1,128)}, u32[]{:S(2)}, u32[]{:S(2)}) async-start(f32[16,3,1,128]{3,2,1,0:T(1,128)} %constant_dynamic-update-slice_fusion.73), calls=%async_computation.5 | async-start | bytes 49152 | tf_op jit(solution)/shard_map/all_to_all | solution.py:12
  464.5 11.4 %scatter_custom_fusion.5 = f32[16384]{0:T(1024)S(1)} fusion(s32[2048]{0:T(1024)} %bitcast.1303, f32[2048]{0:T(1024)S(1)} %bitcast.1310, f32[]{:T(128)} %constant.81.clone.1), kind=kCustom, calls=%fused_computation.864 | custom fusion | flops 2048 | bytes 66048 | tf_op jit(solution)/shard_map/scatter-add | solution.py:80
  478.9 4.7 scatter_fusion.1
  484.5 4.6 copy.867
  495.0 10.9 %gather_fusion.15 = f32[2048,3]{1,0:T(8,128)} fusion(f32[3,16384]{0,1:T(8,128)} %bitcast.1080, s32[2048]{0:T(1024)S(1)} %fusion.272), kind=kCustom, calls=%fused_computation.15 | custom fusion | bytes 57344 | tf_op jit(solution)/shard_map/gather | solution.py:74
  518.4 12.1 %all-to-all-start.6 = ((f32[16,3,1,128]{3,2,1,0:T(1,128)}), f32[16,3,1,128]{3,2,1,0:T(1,128)}, u32[]{:S(2)}, u32[]{:S(2)}) async-start(f32[16,3,1,128]{3,2,1,0:T(1,128)} %constant_dynamic-update-slice_fusion.89), calls=%async_computation.6 | async-start | bytes 49152 | tf_op jit(solution)/shard_map/all_to_all | solution.py:12
  531.8 4.9 collective-permute-start.37
  574.0 11.4 %scatter_custom_fusion.7 = f32[16384]{0:T(1024)S(1)} fusion(s32[2048]{0:T(1024)} %bitcast.1304, f32[2048]{0:T(1024)S(1)} %bitcast.1297, f32[]{:T(128)} %constant.81.clone.1), kind=kCustom, calls=%fused_computation.862 | custom fusion | flops 2048 | bytes 66048 | tf_op jit(solution)/shard_map/scatter-add | solution.py:80
  586.7 4.6 copy.868
  591.3 10.9 %gather_fusion.16 = f32[2048,3]{1,0:T(8,128)} fusion(f32[3,16384]{0,1:T(8,128)} %bitcast.1086, s32[2048]{0:T(1024)S(1)} %fusion.272), kind=kCustom, calls=%fused_computation.16 | custom fusion | bytes 57344 | tf_op jit(solution)/shard_map/gather | solution.py:74
  625.6 11.1 %all-to-all-start.7 = ((f32[16,3,1,128]{3,2,1,0:T(1,128)}), f32[16,3,1,128]{3,2,1,0:T(1,128)S(1)}, u32[]{:S(2)}, u32[]{:S(2)}) async-start(f32[16,3,1,128]{3,2,1,0:T(1,128)} %constant_dynamic-update-slice_fusion.105), calls=%async_computation.7 | async-start | bytes 49152 | tf_op jit(solution)/shard_map/all_to_all | solution.py:12
  644.0 11.6 %scatter_custom_fusion.8 = f32[16384]{0:T(1024)S(1)} fusion(s32[2048]{0:T(1024)} %bitcast.1305, f32[2048]{0:T(1024)S(1)} %bitcast.1314, f32[]{:T(128)} %constant.81.clone.1), kind=kCustom, calls=%fused_computation.860 | custom fusion | flops 2048 | bytes 66048 | tf_op jit(solution)/shard_map/scatter-add | solution.py:80
  661.5 10.9 %gather_fusion.17 = f32[2048,3]{1,0:T(8,128)} fusion(f32[3,16384]{0,1:T(8,128)} %bitcast.1087, s32[2048]{0:T(1024)S(1)} %fusion.272), kind=kCustom, calls=%fused_computation.17 | custom fusion | bytes 57344 | tf_op jit(solution)/shard_map/gather | solution.py:74
  695.8 11.2 %all-to-all-start.8 = ((f32[16,3,1,128]{3,2,1,0:T(1,128)}), f32[16,3,1,128]{3,2,1,0:T(1,128)S(1)}, u32[]{:S(2)}, u32[]{:S(2)}) async-start(f32[16,3,1,128]{3,2,1,0:T(1,128)} %constant_dynamic-update-slice_fusion.121), calls=%async_computation.8 | async-start | bytes 49152 | tf_op jit(solution)/shard_map/all_to_all | solution.py:12
  714.4 11.4 %scatter_custom_fusion.9 = f32[16384]{0:T(1024)S(1)} fusion(s32[2048]{0:T(1024)} %bitcast.1306, f32[2048]{0:T(1024)S(1)} %bitcast.1315, f32[]{:T(128)} %constant.81.clone.1), kind=kCustom, calls=%fused_computation.858 | custom fusion | flops 2048 | bytes 66048 | tf_op jit(solution)/shard_map/scatter-add | solution.py:80
  731.7 10.9 %gather_fusion.18 = f32[2048,3]{1,0:T(8,128)} fusion(f32[3,16384]{0,1:T(8,128)} %bitcast.1088, s32[2048]{0:T(1024)S(1)} %fusion.272), kind=kCustom, calls=%fused_computation.18 | custom fusion | bytes 57344 | tf_op jit(solution)/shard_map/gather | solution.py:74
  765.9 11.2 %all-to-all-start.9 = ((f32[16,3,1,128]{3,2,1,0:T(1,128)}), f32[16,3,1,128]{3,2,1,0:T(1,128)S(1)}, u32[]{:S(2)}, u32[]{:S(2)}) async-start(f32[16,3,1,128]{3,2,1,0:T(1,128)} %constant_dynamic-update-slice_fusion.137), calls=%async_computation.9 | async-start | bytes 49152 | tf_op jit(solution)/shard_map/all_to_all | solution.py:12
  784.5 11.4 %scatter_custom_fusion.10 = f32[16384]{0:T(1024)S(1)} fusion(s32[2048]{0:T(1024)} %bitcast.1307, f32[2048]{0:T(1024)S(1)} %bitcast.1316, f32[]{:T(128)} %constant.81.clone.1), kind=kCustom, calls=%fused_computation.856 | custom fusion | flops 2048 | bytes 66048 | tf_op jit(solution)/shard_map/scatter-add | solution.py:80
  801.8 10.9 %gather_fusion.19 = f32[2048,3]{1,0:T(8,128)} fusion(f32[3,16384]{0,1:T(8,128)} %bitcast.1081, s32[2048]{0:T(1024)S(1)} %fusion.272), kind=kCustom, calls=%fused_computation.19 | custom fusion | bytes 57344 | tf_op jit(solution)/shard_map/gather | solution.py:74
  835.9 11.3 %all-to-all-start.10 = ((f32[16,3,1,128]{3,2,1,0:T(1,128)}), f32[16,3,1,128]{3,2,1,0:T(1,128)}, u32[]{:S(2)}, u32[]{:S(2)}) async-start(f32[16,3,1,128]{3,2,1,0:T(1,128)} %constant_dynamic-update-slice_fusion.153), calls=%async_computation.10 | async-start | bytes 49152 | tf_op jit(solution)/shard_map/all_to_all | solution.py:12
  854.6 11.4 %scatter_custom_fusion.11 = f32[16384]{0:T(1024)S(1)} fusion(s32[2048]{0:T(1024)} %bitcast.1308, f32[2048]{0:T(1024)S(1)} %bitcast.1309, f32[]{:T(128)} %constant.81.clone.1), kind=kCustom, calls=%fused_computation.854 | custom fusion | flops 2048 | bytes 66048 | tf_op jit(solution)/shard_map/scatter-add | solution.py:80
  889.7 9.6 add_reduce_fusion
  901.4 6.7 collective-permute-start.77
  919.9 141.0 %reduce-scatter.2.cloned.1.call-done = f32[2,32]{0,1:T(8,128)} async-done(((f32[2,1024]{0,1:T(8,128)}), f32[2,32]{0,1:T(8,128)}) %reduce-scatter.2.cloned.1.call-update) | async-done | bytes 272 | tf_op jit(solution)/shard_map/reduce_scatter | solution.py:288
  (805 shorter events, 483.4 us)
Async XLA Ops:
  63.0 78.0 %all-to-all-start.1 = ((f32[16,3,1,128]{3,2,1,0:T(1,128)}), f32[16,3,1,128]{3,2,1,0:T(1,128)}, u32[]{:S(2)}, u32[]{:S(2)}) async-start(f32[16,3,1,128]{3,2,1,0:T(1,128)} %constant_dynamic-update-slice_fusion.9), calls=%async_computation.1 | async-start | bytes 49152 | tf_op jit(solution)/shard_map/all_to_all | solution.py:12
  68.0 11.1 %collective-permute-start.2 = (f32[3,1,8,128]{3,2,1,0:T(8,128)S(1)}, f32[3,1,8,128]{3,2,1,0:T(8,128)S(1)}, u32[]{:S(2)}, u32[]{:S(2)}) collective-permute-start(f32[3,1,8,128]{3,2,1,0:T(8,128)S(1)} %get-tuple-element.259), channel_id=1, source_target_pairs={{16,0},{17,1},{18,2},{19,3},{20,4},{21,5},{22,6},{23,7},{24,8},{25... | collective-permute-start | bytes 36872 | tf_op jit(solution)/shard_map/ppermute | solution.py:27
  74.6 61.1 %collective-permute-start = (f32[10,1,8,128]{3,2,1,0:T(8,128)}, f32[10,1,8,128]{3,2,1,0:T(8,128)S(1)}, u32[]{:S(2)}, u32[]{:S(2)}) collective-permute-start(f32[10,1,8,128]{3,2,1,0:T(8,128)} %get-tuple-element.156), channel_id=1, source_target_pairs={{0,16},{1,17},{2,18},{3,19},{4,20},{5,21},{6,22},{7,23},{8,24},{9,... | collective-permute-start | bytes 122888 | tf_op jit(solution)/shard_map/ppermute | solution.py:24
  75.8 59.8 %collective-permute-start.1 = (f32[10,1,8,128]{3,2,1,0:T(8,128)}, f32[10,1,8,128]{3,2,1,0:T(8,128)S(1)}, u32[]{:S(2)}, u32[]{:S(2)}) collective-permute-start(f32[10,1,8,128]{3,2,1,0:T(8,128)} %get-tuple-element.157), channel_id=1, source_target_pairs={{16,0},{17,1},{18,2},{19,3},{20,4},{21,5},{22,6},{23,7},{24,8},{25... | collective-permute-start | bytes 122888 | tf_op jit(solution)/shard_map/ppermute | solution.py:27
  79.8 49.5 %collective-permute-start.6 = (f32[3,18,1,128]{3,2,1,0:T(1,128)}, f32[3,18,1,128]{3,2,1,0:T(1,128)S(1)}, u32[]{:S(2)}, u32[]{:S(2)}) collective-permute-start(f32[3,18,1,128]{3,2,1,0:T(1,128)} %get-tuple-element.229), channel_id=1, source_target_pairs={{4,0},{8,4},{12,8},{5,1},{9,5},{13,9},{6,2},{10,6},{14,10},{7,3},{... | collective-permute-start | bytes 82952 | tf_op jit(solution)/shard_map/ppermute | solution.py:27
  81.1 48.2 %collective-permute-start.7 = (f32[3,18,1,128]{3,2,1,0:T(1,128)}, f32[3,18,1,128]{3,2,1,0:T(1,128)S(1)}, u32[]{:S(2)}, u32[]{:S(2)}) collective-permute-start(f32[3,18,1,128]{3,2,1,0:T(1,128)} %get-tuple-element.228), channel_id=1, source_target_pairs={{0,4},{4,8},{8,12},{1,5},{5,9},{9,13},{2,6},{6,10},{10,14},{3,7},{... | collective-permute-start | bytes 82952 | tf_op jit(solution)/shard_map/ppermute | solution.py:24
  130.4 59.4 %collective-permute-start.10 = (f32[3,18,10,1]{3,2,1,0:T(8,128)}, f32[3,18,10,1]{3,2,1,0:T(8,128)}, u32[]{:S(2)}, u32[]{:S(2)}) collective-permute-start(f32[3,18,10,1]{3,2,1,0:T(8,128)} %get-tuple-element.181), channel_id=1, source_target_pairs={{1,0},{2,1},{3,2},{5,4},{6,5},{7,6},{9,8},{10,9},{11,10},{13,12},{... | collective-permute-start | bytes 6488 | tf_op jit(solution)/shard_map/ppermute | solution.py:27
  131.8 58.0 %collective-permute-start.11 = (f32[3,18,10,1]{3,2,1,0:T(8,128)}, f32[3,18,10,1]{3,2,1,0:T(8,128)}, u32[]{:S(2)}, u32[]{:S(2)}) collective-permute-start(f32[3,18,10,1]{3,2,1,0:T(8,128)} %get-tuple-element.180), channel_id=1, source_target_pairs={{0,1},{1,2},{2,3},{4,5},{5,6},{6,7},{8,9},{9,10},{10,11},{12,13},{... | collective-permute-start | bytes 6488 | tf_op jit(solution)/shard_map/ppermute | solution.py:24
  135.8 31.5 %collective-permute-start.4 = (f32[10,18,1,128]{3,2,1,0:T(1,128)S(1)}, f32[10,18,1,128]{3,2,1,0:T(1,128)S(1)}, u32[]{:S(2)}, u32[]{:S(2)}) collective-permute-start(f32[10,18,1,128]{3,2,1,0:T(1,128)S(1)} %get-tuple-element.154), channel_id=1, source_target_pairs={{0,4},{4,8},{8,12},{1,5},{5,9},{9,13},{2,6},{6,10},{10,14},{3,7},{... | collective-permute-start | bytes 276488 | tf_op jit(solution)/shard_map/ppermute | solution.py:24
  139.6 27.8 %collective-permute-start.5 = (f32[10,18,1,128]{3,2,1,0:T(1,128)S(1)}, f32[10,18,1,128]{3,2,1,0:T(1,128)S(1)}, u32[]{:S(2)}, u32[]{:S(2)}) collective-permute-start(f32[10,18,1,128]{3,2,1,0:T(1,128)S(1)} %get-tuple-element.155), channel_id=1, source_target_pairs={{4,0},{8,4},{12,8},{5,1},{9,5},{13,9},{6,2},{10,6},{14,10},{7,3},{... | collective-permute-start | bytes 276488 | tf_op jit(solution)/shard_map/ppermute | solution.py:27
  141.0 12.8 %all-to-all-start = ((f32[6,16,128]{2,0,1:T(8,128)}), f32[6,16,128]{2,0,1:T(8,128)S(1)}, u32[]{:S(2)}, u32[]{:S(2)}) async-start(f32[6,16,128]{2,0,1:T(8,128)} %bitcast.57), calls=%async_computation | async-start | bytes 131072 | tf_op jit(solution)/shard_map/all_to_all | solution.py:179
  222.8 26.4 %all-to-all-start.2 = ((f32[16,3,1,128]{3,2,1,0:T(1,128)}), f32[16,3,1,128]{3,2,1,0:T(1,128)S(1)}, u32[]{:S(2)}, u32[]{:S(2)}) async-start(f32[16,3,1,128]{3,2,1,0:T(1,128)} %constant_dynamic-update-slice_fusion.25), calls=%async_computation.2 | async-start | bytes 49152 | tf_op jit(solution)/shard_map/all_to_all | solution.py:12
  295.0 18.2 %collective-permute-start.20 = (f32[3,18,1,128]{3,2,1,0:T(1,128)}, f32[3,18,1,128]{3,2,1,0:T(1,128)S(1)}, u32[]{:S(2)}, u32[]{:S(2)}) collective-permute-start(f32[3,18,1,128]{3,2,1,0:T(1,128)} %get-tuple-element.225), channel_id=1, source_target_pairs={{4,0},{8,4},{12,8},{5,1},{9,5},{13,9},{6,2},{10,6},{14,10},{7,3},{... | collective-permute-start | bytes 82952 | tf_op jit(solution)/shard_map/ppermute | solution.py:27
  296.3 16.9 %collective-permute-start.21 = (f32[3,18,1,128]{3,2,1,0:T(1,128)}, f32[3,18,1,128]{3,2,1,0:T(1,128)S(1)}, u32[]{:S(2)}, u32[]{:S(2)}) collective-permute-start(f32[3,18,1,128]{3,2,1,0:T(1,128)} %get-tuple-element.224), channel_id=1, source_target_pairs={{0,4},{4,8},{8,12},{1,5},{5,9},{9,13},{2,6},{6,10},{10,14},{3,7},{... | collective-permute-start | bytes 82952 | tf_op jit(solution)/shard_map/ppermute | solution.py:24
  301.8 18.8 %all-to-all-start.3 = ((f32[16,3,1,128]{3,2,1,0:T(1,128)}), f32[16,3,1,128]{3,2,1,0:T(1,128)}, u32[]{:S(2)}, u32[]{:S(2)}) async-start(f32[16,3,1,128]{3,2,1,0:T(1,128)} %constant_dynamic-update-slice_fusion.41), calls=%async_computation.3 | async-start | bytes 49152 | tf_op jit(solution)/shard_map/all_to_all | solution.py:12
  367.3 17.7 %collective-permute-start.26 = (f32[3,18,1,128]{3,2,1,0:T(1,128)}, f32[3,18,1,128]{3,2,1,0:T(1,128)S(1)}, u32[]{:S(2)}, u32[]{:S(2)}) collective-permute-start(f32[3,18,1,128]{3,2,1,0:T(1,128)} %get-tuple-element.223), channel_id=1, source_target_pairs={{4,0},{8,4},{12,8},{5,1},{9,5},{13,9},{6,2},{10,6},{14,10},{7,3},{... | collective-permute-start | bytes 82952 | tf_op jit(solution)/shard_map/ppermute | solution.py:27
  368.6 16.4 %collective-permute-start.27 = (f32[3,18,1,128]{3,2,1,0:T(1,128)}, f32[3,18,1,128]{3,2,1,0:T(1,128)S(1)}, u32[]{:S(2)}, u32[]{:S(2)}) collective-permute-start(f32[3,18,1,128]{3,2,1,0:T(1,128)} %get-tuple-element.222), channel_id=1, source_target_pairs={{0,4},{4,8},{8,12},{1,5},{5,9},{9,13},{2,6},{6,10},{10,14},{3,7},{... | collective-permute-start | bytes 82952 | tf_op jit(solution)/shard_map/ppermute | solution.py:24
  373.7 18.5 %all-to-all-start.4 = ((f32[16,3,1,128]{3,2,1,0:T(1,128)}), f32[16,3,1,128]{3,2,1,0:T(1,128)}, u32[]{:S(2)}, u32[]{:S(2)}) async-start(f32[16,3,1,128]{3,2,1,0:T(1,128)} %constant_dynamic-update-slice_fusion.57), calls=%async_computation.4 | async-start | bytes 49152 | tf_op jit(solution)/shard_map/all_to_all | solution.py:12
  438.8 17.7 %collective-permute-start.32 = (f32[3,18,1,128]{3,2,1,0:T(1,128)}, f32[3,18,1,128]{3,2,1,0:T(1,128)S(1)}, u32[]{:S(2)}, u32[]{:S(2)}) collective-permute-start(f32[3,18,1,128]{3,2,1,0:T(1,128)} %get-tuple-element.221), channel_id=1, source_target_pairs={{4,0},{8,4},{12,8},{5,1},{9,5},{13,9},{6,2},{10,6},{14,10},{7,3},{... | collective-permute-start | bytes 82952 | tf_op jit(solution)/shard_map/ppermute | solution.py:27
  440.1 16.4 %collective-permute-start.33 = (f32[3,18,1,128]{3,2,1,0:T(1,128)}, f32[3,18,1,128]{3,2,1,0:T(1,128)S(1)}, u32[]{:S(2)}, u32[]{:S(2)}) collective-permute-start(f32[3,18,1,128]{3,2,1,0:T(1,128)} %get-tuple-element.220), channel_id=1, source_target_pairs={{0,4},{4,8},{8,12},{1,5},{5,9},{9,13},{2,6},{6,10},{10,14},{3,7},{... | collective-permute-start | bytes 82952 | tf_op jit(solution)/shard_map/ppermute | solution.py:24
  445.2 18.5 %all-to-all-start.5 = ((f32[16,3,1,128]{3,2,1,0:T(1,128)}), f32[16,3,1,128]{3,2,1,0:T(1,128)}, u32[]{:S(2)}, u32[]{:S(2)}) async-start(f32[16,3,1,128]{3,2,1,0:T(1,128)} %constant_dynamic-update-slice_fusion.73), calls=%async_computation.5 | async-start | bytes 49152 | tf_op jit(solution)/shard_map/all_to_all | solution.py:12
  489.1 58.1 %collective-permute-start.66 = (f32[3,1,8,128]{3,2,1,0:T(8,128)}, f32[3,1,8,128]{3,2,1,0:T(8,128)S(1)}, u32[]{:S(2)}, u32[]{:S(2)}) collective-permute-start(f32[3,1,8,128]{3,2,1,0:T(8,128)} %get-tuple-element.231), channel_id=1, source_target_pairs={{16,0},{17,1},{18,2},{19,3},{20,4},{21,5},{22,6},{23,7},{24,8},{25... | collective-permute-start | bytes 36872 | tf_op jit(solution)/shard_map/ppermute | solution.py:27
  490.4 56.8 %collective-permute-start.67 = (f32[3,1,8,128]{3,2,1,0:T(8,128)}, f32[3,1,8,128]{3,2,1,0:T(8,128)S(1)}, u32[]{:S(2)}, u32[]{:S(2)}) collective-permute-start(f32[3,1,8,128]{3,2,1,0:T(8,128)} %get-tuple-element.230), channel_id=1, source_target_pairs={{0,16},{1,17},{2,18},{3,19},{4,20},{5,21},{6,22},{7,23},{8,24},{9,... | collective-permute-start | bytes 36872 | tf_op jit(solution)/shard_map/ppermute | solution.py:24
  518.4 54.7 %all-to-all-start.6 = ((f32[16,3,1,128]{3,2,1,0:T(1,128)}), f32[16,3,1,128]{3,2,1,0:T(1,128)}, u32[]{:S(2)}, u32[]{:S(2)}) async-start(f32[16,3,1,128]{3,2,1,0:T(1,128)} %constant_dynamic-update-slice_fusion.89), calls=%async_computation.6 | async-start | bytes 49152 | tf_op jit(solution)/shard_map/all_to_all | solution.py:12
  530.5 22.6 %collective-permute-start.36 = (f32[3,1,8,128]{3,2,1,0:T(8,128)S(1)}, f32[3,1,8,128]{3,2,1,0:T(8,128)S(1)}, u32[]{:S(2)}, u32[]{:S(2)}) collective-permute-start(f32[3,1,8,128]{3,2,1,0:T(8,128)S(1)} %get-tuple-element.249), channel_id=1, source_target_pairs={{16,0},{17,1},{18,2},{19,3},{20,4},{21,5},{22,6},{23,7},{24,8},{25... | collective-permute-start | bytes 36872 | tf_op jit(solution)/shard_map/ppermute | solution.py:27
  531.8 21.3 %collective-permute-start.37 = (f32[3,1,8,128]{3,2,1,0:T(8,128)S(1)}, f32[3,1,8,128]{3,2,1,0:T(8,128)S(1)}, u32[]{:S(2)}, u32[]{:S(2)}) collective-permute-start(f32[3,1,8,128]{3,2,1,0:T(8,128)S(1)} %get-tuple-element.248), channel_id=1, source_target_pairs={{0,16},{1,17},{2,18},{3,19},{4,20},{5,21},{6,22},{7,23},{8,24},{9,... | collective-permute-start | bytes 36872 | tf_op jit(solution)/shard_map/ppermute | solution.py:24
  547.2 11.8 %collective-permute-start.68 = (f32[3,18,1,128]{3,2,1,0:T(1,128)S(1)}, f32[3,18,1,128]{3,2,1,0:T(1,128)S(1)}, u32[]{:S(2)}, u32[]{:S(2)}) collective-permute-start(f32[3,18,1,128]{3,2,1,0:T(1,128)S(1)} %get-tuple-element.203), channel_id=1, source_target_pairs={{4,0},{8,4},{12,8},{5,1},{9,5},{13,9},{6,2},{10,6},{14,10},{7,3},{... | collective-permute-start | bytes 82952 | tf_op jit(solution)/shard_map/ppermute | solution.py:27
  548.5 10.5 collective-permute-start.69
  553.2 10.7 %collective-permute-start.38 = (f32[3,18,1,128]{3,2,1,0:T(1,128)S(1)}, f32[3,18,1,128]{3,2,1,0:T(1,128)S(1)}, u32[]{:S(2)}, u32[]{:S(2)}) collective-permute-start(f32[3,18,1,128]{3,2,1,0:T(1,128)S(1)} %get-tuple-element.219), channel_id=1, source_target_pairs={{4,0},{8,4},{12,8},{5,1},{9,5},{13,9},{6,2},{10,6},{14,10},{7,3},{... | collective-permute-start | bytes 82952 | tf_op jit(solution)/shard_map/ppermute | solution.py:27
  559.4 12.6 %collective-permute-start.70 = (f32[3,18,10,1]{3,2,1,0:T(8,128)S(1)}, f32[3,18,10,1]{3,2,1,0:T(8,128)S(1)}, u32[]{:S(2)}, u32[]{:S(2)}) collective-permute-start(f32[3,18,10,1]{3,2,1,0:T(8,128)S(1)} %get-tuple-element.159), channel_id=1, source_target_pairs={{1,0},{2,1},{3,2},{5,4},{6,5},{7,6},{9,8},{10,9},{11,10},{13,12},{... | collective-permute-start | bytes 6488 | tf_op jit(solution)/shard_map/ppermute | solution.py:27
  560.8 11.2 %collective-permute-start.71 = (f32[3,18,10,1]{3,2,1,0:T(8,128)S(1)}, f32[3,18,10,1]{3,2,1,0:T(8,128)S(1)}, u32[]{:S(2)}, u32[]{:S(2)}) collective-permute-start(f32[3,18,10,1]{3,2,1,0:T(8,128)S(1)} %get-tuple-element.158), channel_id=1, source_target_pairs={{0,1},{1,2},{2,3},{4,5},{5,6},{6,7},{8,9},{9,10},{10,11},{12,13},{... | collective-permute-start | bytes 6488 | tf_op jit(solution)/shard_map/ppermute | solution.py:24
  619.2 17.6 %collective-permute-start.44 = (f32[3,18,1,128]{3,2,1,0:T(1,128)S(1)}, f32[3,18,1,128]{3,2,1,0:T(1,128)S(1)}, u32[]{:S(2)}, u32[]{:S(2)}) collective-permute-start(f32[3,18,1,128]{3,2,1,0:T(1,128)S(1)} %get-tuple-element.217), channel_id=1, source_target_pairs={{4,0},{8,4},{12,8},{5,1},{9,5},{13,9},{6,2},{10,6},{14,10},{7,3},{... | collective-permute-start | bytes 82952 | tf_op jit(solution)/shard_map/ppermute | solution.py:27
  620.5 16.3 %collective-permute-start.45 = (f32[3,18,1,128]{3,2,1,0:T(1,128)S(1)}, f32[3,18,1,128]{3,2,1,0:T(1,128)S(1)}, u32[]{:S(2)}, u32[]{:S(2)}) collective-permute-start(f32[3,18,1,128]{3,2,1,0:T(1,128)S(1)} %get-tuple-element.216), channel_id=1, source_target_pairs={{0,4},{4,8},{8,12},{1,5},{5,9},{9,13},{2,6},{6,10},{10,14},{3,7},{... | collective-permute-start | bytes 82952 | tf_op jit(solution)/shard_map/ppermute | solution.py:24
  625.6 18.4 %all-to-all-start.7 = ((f32[16,3,1,128]{3,2,1,0:T(1,128)}), f32[16,3,1,128]{3,2,1,0:T(1,128)S(1)}, u32[]{:S(2)}, u32[]{:S(2)}) async-start(f32[16,3,1,128]{3,2,1,0:T(1,128)} %constant_dynamic-update-slice_fusion.105), calls=%async_computation.7 | async-start | bytes 49152 | tf_op jit(solution)/shard_map/all_to_all | solution.py:12
  689.4 17.7 %collective-permute-start.50 = (f32[3,18,1,128]{3,2,1,0:T(1,128)S(1)}, f32[3,18,1,128]{3,2,1,0:T(1,128)S(1)}, u32[]{:S(2)}, u32[]{:S(2)}) collective-permute-start(f32[3,18,1,128]{3,2,1,0:T(1,128)S(1)} %get-tuple-element.215), channel_id=1, source_target_pairs={{4,0},{8,4},{12,8},{5,1},{9,5},{13,9},{6,2},{10,6},{14,10},{7,3},{... | collective-permute-start | bytes 82952 | tf_op jit(solution)/shard_map/ppermute | solution.py:27
  690.7 16.4 %collective-permute-start.51 = (f32[3,18,1,128]{3,2,1,0:T(1,128)S(1)}, f32[3,18,1,128]{3,2,1,0:T(1,128)S(1)}, u32[]{:S(2)}, u32[]{:S(2)}) collective-permute-start(f32[3,18,1,128]{3,2,1,0:T(1,128)S(1)} %get-tuple-element.214), channel_id=1, source_target_pairs={{0,4},{4,8},{8,12},{1,5},{5,9},{9,13},{2,6},{6,10},{10,14},{3,7},{... | collective-permute-start | bytes 82952 | tf_op jit(solution)/shard_map/ppermute | solution.py:24
  695.8 18.5 %all-to-all-start.8 = ((f32[16,3,1,128]{3,2,1,0:T(1,128)}), f32[16,3,1,128]{3,2,1,0:T(1,128)S(1)}, u32[]{:S(2)}, u32[]{:S(2)}) async-start(f32[16,3,1,128]{3,2,1,0:T(1,128)} %constant_dynamic-update-slice_fusion.121), calls=%async_computation.8 | async-start | bytes 49152 | tf_op jit(solution)/shard_map/all_to_all | solution.py:12
  759.5 17.7 %collective-permute-start.56 = (f32[3,18,1,128]{3,2,1,0:T(1,128)S(1)}, f32[3,18,1,128]{3,2,1,0:T(1,128)S(1)}, u32[]{:S(2)}, u32[]{:S(2)}) collective-permute-start(f32[3,18,1,128]{3,2,1,0:T(1,128)S(1)} %get-tuple-element.213), channel_id=1, source_target_pairs={{4,0},{8,4},{12,8},{5,1},{9,5},{13,9},{6,2},{10,6},{14,10},{7,3},{... | collective-permute-start | bytes 82952 | tf_op jit(solution)/shard_map/ppermute | solution.py:27
  760.8 16.4 %collective-permute-start.57 = (f32[3,18,1,128]{3,2,1,0:T(1,128)S(1)}, f32[3,18,1,128]{3,2,1,0:T(1,128)S(1)}, u32[]{:S(2)}, u32[]{:S(2)}) collective-permute-start(f32[3,18,1,128]{3,2,1,0:T(1,128)S(1)} %get-tuple-element.212), channel_id=1, source_target_pairs={{0,4},{4,8},{8,12},{1,5},{5,9},{9,13},{2,6},{6,10},{10,14},{3,7},{... | collective-permute-start | bytes 82952 | tf_op jit(solution)/shard_map/ppermute | solution.py:24
  765.9 18.5 %all-to-all-start.9 = ((f32[16,3,1,128]{3,2,1,0:T(1,128)}), f32[16,3,1,128]{3,2,1,0:T(1,128)S(1)}, u32[]{:S(2)}, u32[]{:S(2)}) async-start(f32[16,3,1,128]{3,2,1,0:T(1,128)} %constant_dynamic-update-slice_fusion.137), calls=%async_computation.9 | async-start | bytes 49152 | tf_op jit(solution)/shard_map/all_to_all | solution.py:12
  829.5 17.7 %collective-permute-start.62 = (f32[3,18,1,128]{3,2,1,0:T(1,128)S(1)}, f32[3,18,1,128]{3,2,1,0:T(1,128)S(1)}, u32[]{:S(2)}, u32[]{:S(2)}) collective-permute-start(f32[3,18,1,128]{3,2,1,0:T(1,128)S(1)} %get-tuple-element.211), channel_id=1, source_target_pairs={{4,0},{8,4},{12,8},{5,1},{9,5},{13,9},{6,2},{10,6},{14,10},{7,3},{... | collective-permute-start | bytes 82952 | tf_op jit(solution)/shard_map/ppermute | solution.py:27
  830.8 16.5 %collective-permute-start.63 = (f32[3,18,1,128]{3,2,1,0:T(1,128)S(1)}, f32[3,18,1,128]{3,2,1,0:T(1,128)S(1)}, u32[]{:S(2)}, u32[]{:S(2)}) collective-permute-start(f32[3,18,1,128]{3,2,1,0:T(1,128)S(1)} %get-tuple-element.210), channel_id=1, source_target_pairs={{0,4},{4,8},{8,12},{1,5},{5,9},{9,13},{2,6},{6,10},{10,14},{3,7},{... | collective-permute-start | bytes 82952 | tf_op jit(solution)/shard_map/ppermute | solution.py:24
  835.9 17.9 %all-to-all-start.10 = ((f32[16,3,1,128]{3,2,1,0:T(1,128)}), f32[16,3,1,128]{3,2,1,0:T(1,128)}, u32[]{:S(2)}, u32[]{:S(2)}) async-start(f32[16,3,1,128]{3,2,1,0:T(1,128)} %constant_dynamic-update-slice_fusion.153), calls=%async_computation.10 | async-start | bytes 49152 | tf_op jit(solution)/shard_map/all_to_all | solution.py:12
  847.2 213.6 %reduce-scatter.2.cloned.1.call-start = ((), (), s32[]{:S(2)}) async-start(), calls=%async_computation.12 | async-start | bytes 540672 | tf_op jit(solution)/shard_map/reduce_scatter | solution.py:288
  867.3 16.5 %collective-permute-start.72 = (f32[3,1,8,128]{3,2,1,0:T(8,128)S(1)}, f32[3,1,8,128]{3,2,1,0:T(8,128)S(1)}, u32[]{:S(2)}, u32[]{:S(2)}) collective-permute-start(f32[3,1,8,128]{3,2,1,0:T(8,128)S(1)} %get-tuple-element.233), channel_id=1, source_target_pairs={{16,0},{17,1},{18,2},{19,3},{20,4},{21,5},{22,6},{23,7},{24,8},{25... | collective-permute-start | bytes 36872 | tf_op jit(solution)/shard_map/ppermute | solution.py:27
  868.8 15.0 %collective-permute-start.73 = (f32[3,1,8,128]{3,2,1,0:T(8,128)S(1)}, f32[3,1,8,128]{3,2,1,0:T(8,128)S(1)}, u32[]{:S(2)}, u32[]{:S(2)}) collective-permute-start(f32[3,1,8,128]{3,2,1,0:T(8,128)S(1)} %get-tuple-element.232), channel_id=1, source_target_pairs={{0,16},{1,17},{2,18},{3,19},{4,20},{5,21},{6,22},{7,23},{8,24},{9,... | collective-permute-start | bytes 36872 | tf_op jit(solution)/shard_map/ppermute | solution.py:24
  883.9 15.6 %collective-permute-start.74 = (f32[3,18,1,128]{3,2,1,0:T(1,128)S(1)}, f32[3,18,1,128]{3,2,1,0:T(1,128)S(1)}, u32[]{:S(2)}, u32[]{:S(2)}) collective-permute-start(f32[3,18,1,128]{3,2,1,0:T(1,128)S(1)} %get-tuple-element.209), channel_id=1, source_target_pairs={{4,0},{8,4},{12,8},{5,1},{9,5},{13,9},{6,2},{10,6},{14,10},{7,3},{... | collective-permute-start | bytes 82952 | tf_op jit(solution)/shard_map/ppermute | solution.py:27
  885.2 14.3 %collective-permute-start.75 = (f32[3,18,1,128]{3,2,1,0:T(1,128)S(1)}, f32[3,18,1,128]{3,2,1,0:T(1,128)S(1)}, u32[]{:S(2)}, u32[]{:S(2)}) collective-permute-start(f32[3,18,1,128]{3,2,1,0:T(1,128)S(1)} %get-tuple-element.208), channel_id=1, source_target_pairs={{0,4},{4,8},{8,12},{1,5},{5,9},{9,13},{2,6},{6,10},{10,14},{3,7},{... | collective-permute-start | bytes 82952 | tf_op jit(solution)/shard_map/ppermute | solution.py:24
  (155 other events, 1901.9 us)
Sparse Core Ops, SparseCore 0:
  919.2 141.5 reduce-scatter.1
